TPU v7x, 512 devices: a whole 4x8x8 slice. The times are simulated.
512 devices in a mesh: gx: 16 (over z_lo, y), gy: 32 (over x, z_hi, core).
Axes of the slice: x: 4, y: 8, z: 8 (z_hi: 4, z_lo: 2; z = z_hi * 2 + z_lo), core: 2. Of those that a mesh axis runs over, the one named last changes fastest.
Arguments:
- displacement: bfloat16 [3, 16, 256, 2048], P(None, None, 'gy', 'gx'), may hold values from -6 to 6
- density: float32 [16, 256, 2048], P(None, 'gy', 'gx'), may hold values from 0.3 to 1
- solid: int32 [16, 256, 2048], P(None, 'gy', 'gx'), may hold values 0 or 1
- fixed_nodes: int32 [4096], replicated, may hold values from 0 to 8388607
- load_nodes: int32 [512], replicated, may hold values from 0 to 8388607
- load_forces: float32 [512, 3], replicated, may hold values from -6 to 6
Outputs:
- smoothed: bfloat16 [3, 16, 256, 2048], P(None, None, 'gy', 'gx')
- filtered: float32 [16, 256, 2048], P(None, 'gy', 'gx')
Inputs may be any that keep to these rules, and one draw needn't show every extreme that they name: `fixed_nodes`: global node indices; a node may appear more than once. `load_nodes`: global node indices; forces at a repeated node add up.
All inputs are finite; a program needn't handle non-finite values. No bound on the sum of `solid` on one device may be relied on, other than what follows from the above.
Results may differ from a plain program's by a relative error of at most 0.0092.
Values may be sent and summed in bfloat16 or wider, within the bound.
No kernel may reach another device: no remote copies, remote signals or barrier semaphores. Data moves between devices by JAX's collectives and lax.ppermute only.
A program may use at most 64 MiB of HBM per device.

v0:
```python
import math

import jax
import jax.numpy as jnp
import numpy as np
from jax import lax
from jax.sharding import PartitionSpec as P

void_modulus = 0.001
spectral_mid = 1.375
spectral_half = 1.125


def passed_along(shard, axis, by):
    size = lax.axis_size(axis)
    pairs = [(i, i + by) for i in range(size) if 0 <= i + by < size]
    return lax.ppermute(shard, axis, pairs)


def extended(block, sides, width):
    for axis, dim in sides:
        count = lax.axis_size(axis)
        forward = [(i, i + 1) for i in range(count - 1)]
        backward = [(target, source) for source, target in forward]
        low = lax.ppermute(
            lax.slice_in_dim(block, block.shape[dim] - width, None, axis=dim), axis, forward
        )
        high = lax.ppermute(lax.slice_in_dim(block, 0, width, axis=dim), axis, backward)
        block = jnp.concatenate([low, block, high], axis=dim)
    return block


def stiffness_table():
    poisson = 0.3
    lame = poisson / ((1.0 + poisson) * (1.0 - 2.0 * poisson))
    shear = 0.5 / (1.0 + poisson)
    elastic = np.zeros((6, 6))
    elastic[:3, :3] = lame
    for index in range(3):
        elastic[index, index] += 2.0 * shear
        elastic[index + 3, index + 3] = shear
    points = [0.5 - 0.5 / math.sqrt(3.0), 0.5 + 0.5 / math.sqrt(3.0)]
    table = np.zeros((24, 24))
    for point_z in points:
        for point_y in points:
            for point_x in points:
                strain = np.zeros((6, 24))
                for corner in range(8):
                    bit_z, bit_y, bit_x = (corner // 4, corner // 2 % 2, corner % 2)
                    shape_x = point_x if bit_x else 1.0 - point_x
                    shape_y = point_y if bit_y else 1.0 - point_y
                    shape_z = point_z if bit_z else 1.0 - point_z
                    slope_x = 1.0 if bit_x else -1.0
                    slope_y = 1.0 if bit_y else -1.0
                    slope_z = 1.0 if bit_z else -1.0
                    grad_x = slope_x * shape_y * shape_z
                    grad_y = shape_x * slope_y * shape_z
                    grad_z = shape_x * shape_y * slope_z
                    strain[0, corner] = grad_x
                    strain[1, 8 + corner] = grad_y
                    strain[2, 16 + corner] = grad_z
                    strain[3, corner] = grad_y
                    strain[3, 8 + corner] = grad_x
                    strain[4, 8 + corner] = grad_z
                    strain[4, 16 + corner] = grad_y
                    strain[5, corner] = grad_z
                    strain[5, 16 + corner] = grad_x
                table += strain.T @ elastic @ strain / 8.0
    return table


def conic_taps():
    taps = []
    for shift_z in range(-2, 3):
        for shift_y in range(-2, 3):
            for shift_x in range(-2, 3):
                weight = 3.0 - math.sqrt(shift_z * shift_z + shift_y * shift_y + shift_x * shift_x)
                if weight > 0.0:
                    taps.append((shift_z, shift_y, shift_x, weight))
    return taps


def conic_filter(padded, depth, rows, columns):
    total = jnp.zeros((depth, rows, columns), jnp.float32)
    for shift_z, shift_y, shift_x, weight in conic_taps():
        total = (
            total
            + weight
            * padded[
                2 + shift_z : 2 + shift_z + depth,
                2 + shift_y : 2 + shift_y + rows,
                2 + shift_x : 2 + shift_x + columns,
            ]
        )
    return total


def exists_region(z_low, z_count, y_low, rows, x_low, columns, depth, grid_y, grid_x):
    zpos = z_low + jnp.arange(z_count, dtype=jnp.int32)
    ypos = y_low + jnp.arange(rows, dtype=jnp.int32)
    xpos = x_low + jnp.arange(columns, dtype=jnp.int32)
    inside_z = ((zpos >= 0) & (zpos < depth - 1))[:, None, None]
    inside_y = ((ypos >= 0) & (ypos < grid_y - 1))[None, :, None]
    inside_x = ((xpos >= 0) & (xpos < grid_x - 1))[None, None, :]
    return (inside_z & inside_y & inside_x).astype(jnp.float32)


def element_terms(upper, table_low, depth, rows, columns):
    padded = jnp.pad(upper, ((0, 0), (0, 1), (0, 0), (0, 0)))
    stacked = jnp.stack(
        [
            padded[
                component,
                depth_bit : depth_bit + depth,
                row_bit : row_bit + rows,
                col_bit : col_bit + columns,
            ]
            for component in range(3)
            for depth_bit in (0, 1)
            for row_bit in (0, 1)
            for col_bit in (0, 1)
        ]
    )
    product = jnp.einsum("kj,jzyx->kzyx", table_low, stacked, preferred_element_type=jnp.float32)
    return (stacked, product)


def group_depth(terms):
    count = terms.shape[0] // 8
    split = terms.reshape((count, 2, 2, 2) + tuple(terms.shape[1:]))
    high = split[:, 1]
    moved = jnp.concatenate([jnp.zeros_like(high[:, :, :, :1]), high[:, :, :, :-1]], axis=3)
    return split[:, 0] + moved


def upper_rim(field):
    column = passed_along(field[:, :, :, :1], "gx", -1)
    widened = jnp.concatenate([field, column], axis=3)
    row = passed_along(widened[:, :, :1, :], "gy", -1)
    return jnp.concatenate([widened, row], axis=2)


def assemble_lower(grouped):
    column = passed_along(grouped[:, :, 1, :, :, -1:], "gx", 1)
    moved = jnp.concatenate([column, grouped[:, :, 1, :, :, :-1]], axis=-1)
    partial_sum = grouped[:, :, 0] + moved
    row = passed_along(partial_sum[:, 1, :, -1:, :], "gy", 1)
    lifted = jnp.concatenate([row, partial_sum[:, 1, :, :-1, :]], axis=2)
    return partial_sum[:, 0] + lifted


def shards(displacement, density, solid, fixed_nodes, load_nodes, load_forces):
    depth, rows, columns = density.shape
    grid_y = rows * lax.axis_size("gy")
    grid_x = columns * lax.axis_size("gx")
    y_start = lax.axis_index("gy") * rows
    x_start = lax.axis_index("gx") * columns
    table_low = jnp.asarray(stiffness_table(), jnp.float32).astype(jnp.bfloat16)
    diag_terms = jnp.diagonal(lax.optimization_barrier(table_low).astype(jnp.float32))
    exists = exists_region(0, depth, y_start, rows, x_start, columns, depth, grid_y, grid_x)
    designed = (1 - solid).astype(jnp.float32)
    physical = jnp.where(solid == 1, jnp.float32(1.0), density)
    stiffness = (void_modulus + (1.0 - void_modulus) * physical**3) * exists
    coefficient = -3.0 * (1.0 - void_modulus) * physical * physical * exists * designed
    fixed_x = fixed_nodes % grid_x - x_start
    fixed_y = fixed_nodes // grid_x % grid_y - y_start
    fixed_z = fixed_nodes // (grid_x * grid_y)
    fixed_in = (fixed_x >= 0) & (fixed_x < columns) & (fixed_y >= 0) & (fixed_y < rows)
    free = (
        jnp.ones((depth, rows, columns), jnp.float32)
        .at[fixed_z, jnp.where(fixed_in, fixed_y, rows), jnp.where(fixed_in, fixed_x, columns)]
        .set(0.0, mode="drop")
    )
    load_x = load_nodes % grid_x - x_start
    load_y = load_nodes // grid_x % grid_y - y_start
    load_z = load_nodes // (grid_x * grid_y)
    load_in = (load_x >= 0) & (load_x < columns) & (load_y >= 0) & (load_y < rows)
    loads = (
        jnp.zeros((3, depth, rows, columns), jnp.float32)
        .at[:, load_z, jnp.where(load_in, load_y, rows), jnp.where(load_in, load_x, columns)]
        .add(load_forces.T, mode="drop")
    )

    def operate(field, with_diag):
        upper = upper_rim(field)
        stacked, product = element_terms(upper, table_low, depth, rows, columns)
        terms = product * stiffness
        if with_diag:
            terms = jnp.concatenate([terms, diag_terms[:, None, None, None] * stiffness], axis=0)
        return assemble_lower(group_depth(terms))

    sigma = spectral_mid / spectral_half
    first = 1.0 / sigma
    second = 1.0 / (2.0 * sigma - first)
    both = operate(displacement, True)
    applied = both[:3]
    diagonal = both[3:]
    residual0 = (loads - applied) * free
    step0 = (residual0 / (spectral_mid * diagonal)).astype(jnp.bfloat16)
    applied1 = operate(step0, False)
    residual1 = residual0 - applied1 * free
    step1 = (
        second * first * step0.astype(jnp.float32)
        + 2.0 * second / spectral_half * residual1 / diagonal
    )
    smoothed = (displacement.astype(jnp.float32) + step0.astype(jnp.float32) + step1).astype(
        jnp.bfloat16
    )
    upper = upper_rim(smoothed)
    stacked, product = element_terms(upper, table_low, depth, rows, columns)
    sensitivity = coefficient * jnp.sum(stacked * product, axis=0)
    weight_sum = conic_filter(
        exists_region(
            -2, depth + 4, y_start - 2, rows + 4, x_start - 2, columns + 4, depth, grid_y, grid_x
        ),
        depth,
        rows,
        columns,
    )
    alive = exists > 0
    ratio = jnp.where(alive, sensitivity / jnp.where(alive, weight_sum, 1.0), 0.0)
    ratio_cycle = extended(ratio, (("gx", 2), ("gy", 1)), 2)
    padded = jnp.pad(ratio_cycle, ((2, 2), (0, 0), (0, 0)))
    filtered = conic_filter(padded, depth, rows, columns) * exists * designed
    return (smoothed, filtered)


def solution(mesh):
    placed = (P(None, None, "gy", "gx"), P(None, "gy", "gx"), P(None, "gy", "gx"), P(), P(), P())
    return jax.shard_map(
        shards,
        mesh=mesh,
        in_specs=placed,
        out_specs=(P(None, None, "gy", "gx"), P(None, "gy", "gx")),
        check_vma=False,
    )
```

profile of v0, /device:TPU:60, one launch (start us, length us, event | category | flops | bytes accessed | tf_op | source)
XLA Modules:
  0.0 225.2 jit_solution(7510104334533122866)
XLA Ops:
  1.6 3.3 %collective-permute-start = (bf16[3,16,8,1]{3,0,2,1:T(4,128)(2,1)S(1)}, bf16[3,16,8,1]{3,0,2,1:T(4,128)(2,1)S(1)}, u32[]{:S(2)}, u32[]{:S(2)}) collective-permute-start(bf16[3,16,8,1]{3,0,2,1:T(4,128)(2,1)S(1)} %copy.80), channel_id=1, source_target_pairs={{32,0},{64,32},{96,64},{128,96},{160,128},{192,160},{224,192},{256... | collective-permute-start | bytes 2312 | tf_op jit(solution)/shard_map/ppermute | solution.py:17
  16.3 4.3 %broadcast_in_dim.32 = f32[3,16,8,128]{0,3,2,1:T(8,128)} broadcast(f32[]{:T(128)} %constant.137.clone.1), dimensions={} | broadcast | bytes 196612 | tf_op jit(solution)/shard_map/broadcast_in_dim | solution.py:179
  20.6 50.9 %scatter_fusion = f32[3,16,8,128]{0,3,2,1:T(8,128)} fusion(f32[3,16,8,128]{0,3,2,1:T(8,128)} %broadcast_in_dim.32, s32[512]{0:T(512)S(1)} %bitcast.84, f32[512,3]{1,0:T(8,128)S(1)} %copy.46), kind=kCustom, calls=%fused_computation.1 | custom fusion | flops 1536 | bytes 24576 | tf_op jit(solution)/shard_map/scatter-add | solution.py:181
  71.5 5.2 %copy.57 = f32[3,16,8,128]{3,0,2,1:T(4,128)S(1)} copy(f32[3,16,8,128]{0,3,2,1:T(8,128)} %scatter_fusion) | data formatting | bytes 393216 | tf_op jit(solution)/shard_map/scatter-add | solution.py:181
  76.8 15.6 %scatter_custom_fusion.1 = f32[16384]{0:T(1024)S(1)} fusion(s32[4096]{0:T(1024)S(1)} %broadcast_select_fusion, f32[4096]{0:T(1024)S(1)} %broadcast.311, f32[]{:T(128)} %constant.156.clone.1), kind=kCustom, calls=%fused_computation.476 | custom fusion | bytes 65540
  92.5 9.3 %collective-permute-start.1 = (bf16[3,16,1,129]{3,0,2,1:T(4,128)(2,1)S(1)}, bf16[3,16,1,129]{3,0,2,1:T(4,128)(2,1)S(1)}, u32[]{:S(2)}, u32[]{:S(2)}) collective-permute-start(bf16[3,16,1,129]{3,0,2,1:T(4,128)(2,1)S(1)} %slice.1274), channel_id=1, source_target_pairs={{1,0},{2,1},{3,2},{4,3},{5,4},{6,5},{7,6},{8,7},{9,8},{10,9},{11,1... | collective-permute-start | bytes 37160 | tf_op jit(solution)/shard_map/ppermute | solution.py:17
  106.3 4.9 %stack.9 = bf16[24,16,8,128]{3,0,2,1:T(8,128)(2,1)S(1)} concatenate(bf16[1,16,8,128]{3,0,2,1:T(2,128)(2,1)} %copy.79, bf16[1,16,8,128]{3,0,2,1:T(2,128)(2,1)} %get-tuple-element.78, bf16[1,16,8,128]{3,0,2,1:T(2,128)(2,1)} %get-tuple-element.65, bf16[1,16,8,128]{3,0,2,1:T(2,128)(2,1)} %get-tuple-element.66, bf16[1,16,8,128]{3,0,2,1:T(2,128)(2,1)S(1)} %get-tuple-element.63, ...), dimensions={0} | concatenate | bytes 1572864 | tf_op jit(solution)/shard_map/stack | solution.py:110
  116.2 5.0 %collective-permute-start.2 = (f32[6,2,16,8,1]{2,3,4,1,0:T(8,128)}, f32[6,2,16,8,1]{2,3,4,1,0:T(8,128)}, u32[]{:S(2)}, u32[]{:S(2)}) collective-permute-start(f32[6,2,16,8,1]{2,3,4,1,0:T(8,128)} %bitcast.102), channel_id=1, source_target_pairs={{0,32},{32,64},{64,96},{96,128},{128,160},{160,192},{192,224},{224... | collective-permute-start | bytes 18440 | tf_op jit(solution)/shard_map/ppermute | solution.py:17
  123.1 2.7 %copy.55 = f32[6,2,16,8,1]{4,0,3,2,1:T(8,128)} copy(f32[6,2,16,8,1]{2,3,4,1,0:T(8,128)} %collective-permute-done.2) | data formatting | bytes 12288 | tf_op jit(solution)/shard_map/ppermute | solution.py:17
  129.4 6.6 %collective-permute-done.3 = f32[6,16,1,128]{3,0,1,2:T(8,128)S(1)} collective-permute-done((f32[6,16,1,128]{3,0,1,2:T(8,128)S(1)}, f32[6,16,1,128]{3,0,1,2:T(8,128)S(1)}, u32[]{:S(2)}, u32[]{:S(2)}) %collective-permute-start.3) | collective-permute-done | bytes 49184 | tf_op jit(solution)/shard_map/ppermute | solution.py:17
  136.3 2.2 collective-permute-start.4
  139.0 6.9 %collective-permute-done.4 = bf16[3,16,8,1]{3,0,2,1:T(4,128)(2,1)S(1)} collective-permute-done((bf16[3,16,8,1]{3,0,2,1:T(4,128)(2,1)S(1)}, bf16[3,16,8,1]{3,0,2,1:T(4,128)(2,1)S(1)}, u32[]{:S(2)}, u32[]{:S(2)}) %collective-permute-start.4) | collective-permute-done | bytes 800 | tf_op jit(solution)/shard_map/ppermute | solution.py:17
  151.1 2.6 %stack.10 = bf16[24,16,8,128]{3,0,2,1:T(8,128)(2,1)S(1)} concatenate(bf16[1,16,8,128]{3,0,2,1:T(2,128)(2,1)S(1)} %get-tuple-element.88, bf16[1,16,8,128]{3,0,2,1:T(2,128)(2,1)S(1)} %get-tuple-element.74, bf16[1,16,8,128]{3,0,2,1:T(2,128)(2,1)S(1)} %get-tuple-element.51, bf16[1,16,8,128]{3,0,2,1:T(2,128)(2,1)S(1)} %get-tuple-element.50, ...), dimensions={0} | concatenate | bytes 1572864 | tf_op jit(solution)/shard_map/stack | solution.py:110
  157.1 3.6 %collective-permute-start.6 = (f32[3,2,16,8,1]{4,0,3,2,1:T(4,128)S(1)}, f32[3,2,16,8,1]{4,0,3,2,1:T(4,128)S(1)}, u32[]{:S(2)}, u32[]{:S(2)}) collective-permute-start(f32[3,2,16,8,1]{4,0,3,2,1:T(4,128)S(1)} %copy.61), channel_id=1, source_target_pairs={{0,32},{32,64},{64,96},{96,128},{128,160},{160,192},{192,224},{224... | collective-permute-start | bytes 9224 | tf_op jit(solution)/shard_map/ppermute | solution.py:17
  160.8 11.7 %collective-permute-done.6 = f32[3,2,16,8,1]{4,0,3,2,1:T(4,128)S(1)} collective-permute-done((f32[3,2,16,8,1]{4,0,3,2,1:T(4,128)S(1)}, f32[3,2,16,8,1]{4,0,3,2,1:T(4,128)S(1)}, u32[]{:S(2)}, u32[]{:S(2)}) %collective-permute-start.6) | collective-permute-done | bytes 3104 | tf_op jit(solution)/shard_map/ppermute | solution.py:17
  174.9 6.3 %collective-permute-done.7 = f32[3,16,1,128]{3,0,1,2:T(4,128)S(1)} collective-permute-done((f32[3,16,1,128]{3,0,1,2:T(4,128)S(1)}, f32[3,16,1,128]{3,0,1,2:T(4,128)S(1)}, u32[]{:S(2)}, u32[]{:S(2)}) %collective-permute-start.7) | collective-permute-done | bytes 24608 | tf_op jit(solution)/shard_map/ppermute | solution.py:17
  183.6 7.0 %collective-permute-done.8 = bf16[3,16,8,1]{3,0,2,1:T(4,128)(2,1)S(1)} collective-permute-done((bf16[3,16,8,1]{3,0,2,1:T(4,128)(2,1)S(1)}, bf16[3,16,8,1]{3,0,2,1:T(4,128)(2,1)S(1)}, u32[]{:S(2)}, u32[]{:S(2)}) %collective-permute-start.8) | collective-permute-done | bytes 800 | tf_op jit(solution)/shard_map/ppermute | solution.py:17
  190.6 2.1 collective-permute-start.9
  195.9 2.6 %stack.11 = bf16[24,16,8,128]{3,0,2,1:T(8,128)(2,1)S(1)} concatenate(bf16[1,16,8,128]{3,0,2,1:T(2,128)(2,1)S(1)} %get-tuple-element.85, bf16[1,16,8,128]{3,0,2,1:T(2,128)(2,1)S(1)} %get-tuple-element.71, bf16[1,16,8,128]{3,0,2,1:T(2,128)(2,1)S(1)} %get-tuple-element.33, bf16[1,16,8,128]{3,0,2,1:T(2,128)(2,1)S(1)} %get-tuple-element.32, ...), dimensions={0} | concatenate | bytes 1572864 | tf_op jit(solution)/shard_map/stack | solution.py:110
  200.4 3.6 %collective-permute-start.10 = (f32[16,8,2]{2,1,0:T(8,128)S(1)}, f32[16,8,2]{2,1,0:T(8,128)S(1)}, u32[]{:S(2)}, u32[]{:S(2)}) collective-permute-start(f32[16,8,2]{2,1,0:T(8,128)S(1)} %get-tuple-element.92), channel_id=1, source_target_pairs={{0,32},{32,64},{64,96},{96,128},{128,160},{160,192},{192,224},{224... | collective-permute-start | bytes 3080 | tf_op jit(solution)/shard_map/ppermute | solution.py:25
  204.1 2.2 collective-permute-start.11
  206.6 5.7 %collective-permute-done.11 = f32[16,8,2]{2,1,0:T(8,128)S(1)} collective-permute-done((f32[16,8,2]{2,1,0:T(8,128)S(1)}, f32[16,8,2]{2,1,0:T(8,128)S(1)}, u32[]{:S(2)}, u32[]{:S(2)}) %collective-permute-start.11) | collective-permute-done | bytes 1056 | tf_op jit(solution)/shard_map/ppermute | solution.py:28
  214.4 6.7 %collective-permute-start.13 = (f32[16,2,132]{2,1,0:T(2,128)S(1)}, f32[16,2,132]{2,1,0:T(2,128)S(1)}, u32[]{:S(2)}, u32[]{:S(2)}) collective-permute-start(f32[16,2,132]{2,1,0:T(2,128)S(1)} %get-tuple-element.82), channel_id=1, source_target_pairs={{1,0},{2,1},{3,2},{4,3},{5,4},{6,5},{7,6},{8,7},{9,8},{10,9},{11,1... | collective-permute-start | bytes 50696 | tf_op jit(solution)/shard_map/ppermute | solution.py:28
  223.1 2.1 fusion.34
  (110 shorter events, 50.7 us)
Async XLA Ops:
  1.6 90.7 %collective-permute-start = (bf16[3,16,8,1]{3,0,2,1:T(4,128)(2,1)S(1)}, bf16[3,16,8,1]{3,0,2,1:T(4,128)(2,1)S(1)}, u32[]{:S(2)}, u32[]{:S(2)}) collective-permute-start(bf16[3,16,8,1]{3,0,2,1:T(4,128)(2,1)S(1)} %copy.80), channel_id=1, source_target_pairs={{32,0},{64,32},{96,64},{128,96},{160,128},{192,160},{224,192},{256... | collective-permute-start | bytes 2312 | tf_op jit(solution)/shard_map/ppermute | solution.py:17
  5.9 10.3 %copy-start.4 = (f32[512,3]{0,1:T(4,128)S(1)}, f32[512,3]{0,1:T(4,128)}, u32[]{:S(2)}) copy-start(f32[512,3]{0,1:T(4,128)} %param.12) | copy-start | bytes 18436
  6.7 9.6 %copy-start.5 = (pred[128]{0:T(512)(128)(4,1)}, pred[128]{0:T(512)(128)(4,1)S(1)}, u32[]{:S(2)}) copy-start(pred[128]{0:T(512)(128)(4,1)S(1)} %compare_and_fusion.4) | copy-start | bytes 388
  92.5 10.9 %collective-permute-start.1 = (bf16[3,16,1,129]{3,0,2,1:T(4,128)(2,1)S(1)}, bf16[3,16,1,129]{3,0,2,1:T(4,128)(2,1)S(1)}, u32[]{:S(2)}, u32[]{:S(2)}) collective-permute-start(bf16[3,16,1,129]{3,0,2,1:T(4,128)(2,1)S(1)} %slice.1274), channel_id=1, source_target_pairs={{1,0},{2,1},{3,2},{4,3},{5,4},{6,5},{7,6},{8,7},{9,8},{10,9},{11,1... | collective-permute-start | bytes 37160 | tf_op jit(solution)/shard_map/ppermute | solution.py:17
  104.7 6.5 %copy-start.3 = (bf16[24,24,1,1]{1,0,3,2:T(8,128)(2,1)S(1)}, bf16[24,24,1,1]{1,0,3,2:T(8,128)(2,1)}, u32[]{:S(2)}) copy-start(bf16[24,24,1,1]{1,0,3,2:T(8,128)(2,1)} %constant.231) | copy-start | bytes 3460
  116.2 6.9 %collective-permute-start.2 = (f32[6,2,16,8,1]{2,3,4,1,0:T(8,128)}, f32[6,2,16,8,1]{2,3,4,1,0:T(8,128)}, u32[]{:S(2)}, u32[]{:S(2)}) collective-permute-start(f32[6,2,16,8,1]{2,3,4,1,0:T(8,128)} %bitcast.102), channel_id=1, source_target_pairs={{0,32},{32,64},{64,96},{96,128},{128,160},{160,192},{192,224},{224... | collective-permute-start | bytes 18440 | tf_op jit(solution)/shard_map/ppermute | solution.py:17
  127.4 8.6 %collective-permute-start.3 = (f32[6,16,1,128]{3,0,1,2:T(8,128)S(1)}, f32[6,16,1,128]{3,0,1,2:T(8,128)S(1)}, u32[]{:S(2)}, u32[]{:S(2)}) collective-permute-start(f32[6,16,1,128]{3,0,1,2:T(8,128)S(1)} %slice_bitcast_fusion.8), channel_id=1, source_target_pairs={{0,1},{1,2},{2,3},{3,4},{4,5},{5,6},{6,7},{7,8},{8,9},{9,10},{10,1... | collective-permute-start | bytes 147464 | tf_op jit(solution)/shard_map/ppermute | solution.py:17
  136.3 9.6 %collective-permute-start.4 = (bf16[3,16,8,1]{3,0,2,1:T(4,128)(2,1)S(1)}, bf16[3,16,8,1]{3,0,2,1:T(4,128)(2,1)S(1)}, u32[]{:S(2)}, u32[]{:S(2)}) collective-permute-start(bf16[3,16,8,1]{3,0,2,1:T(4,128)(2,1)S(1)} %bitcast.88), channel_id=1, source_target_pairs={{32,0},{64,32},{96,64},{128,96},{160,128},{192,160},{224,192},{256... | collective-permute-start | bytes 2312 | tf_op jit(solution)/shard_map/ppermute | solution.py:17
  145.9 3.5 %collective-permute-start.5 = (bf16[3,16,1,129]{3,0,2,1:T(4,128)(2,1)S(1)}, bf16[3,16,1,129]{3,0,2,1:T(4,128)(2,1)S(1)}, u32[]{:S(2)}, u32[]{:S(2)}) collective-permute-start(bf16[3,16,1,129]{3,0,2,1:T(4,128)(2,1)S(1)} %fusion.215), channel_id=1, source_target_pairs={{1,0},{2,1},{3,2},{4,3},{5,4},{6,5},{7,6},{8,7},{9,8},{10,9},{11,1... | collective-permute-start | bytes 37160 | tf_op jit(solution)/shard_map/ppermute | solution.py:17
  157.1 15.5 %collective-permute-start.6 = (f32[3,2,16,8,1]{4,0,3,2,1:T(4,128)S(1)}, f32[3,2,16,8,1]{4,0,3,2,1:T(4,128)S(1)}, u32[]{:S(2)}, u32[]{:S(2)}) collective-permute-start(f32[3,2,16,8,1]{4,0,3,2,1:T(4,128)S(1)} %copy.61), channel_id=1, source_target_pairs={{0,32},{32,64},{64,96},{96,128},{128,160},{160,192},{192,224},{224... | collective-permute-start | bytes 9224 | tf_op jit(solution)/shard_map/ppermute | solution.py:17
  160.8 20.4 %copy-start = (bf16[3,16,8,128]{3,2,1,0:T(8,128)(2,1)S(1)}, bf16[3,16,8,128]{3,2,1,0:T(8,128)(2,1)}, u32[]{:S(2)}) copy-start(bf16[3,16,8,128]{3,2,1,0:T(8,128)(2,1)} %param.7) | copy-start | bytes 294916
  172.9 10.5 %copy-start.7 = (pred[132]{0:T(512)(128)(4,1)S(1)}, pred[132]{0:T(512)(128)(4,1)}, u32[]{:S(2)}) copy-start(pred[132]{0:T(512)(128)(4,1)} %compare_and_fusion.1) | copy-start | bytes 400
  173.0 8.2 %collective-permute-start.7 = (f32[3,16,1,128]{3,0,1,2:T(4,128)S(1)}, f32[3,16,1,128]{3,0,1,2:T(4,128)S(1)}, u32[]{:S(2)}, u32[]{:S(2)}) collective-permute-start(f32[3,16,1,128]{3,0,1,2:T(4,128)S(1)} %slice_bitcast_fusion.9), channel_id=1, source_target_pairs={{0,1},{1,2},{2,3},{3,4},{4,5},{5,6},{6,7},{7,8},{8,9},{9,10},{10,1... | collective-permute-start | bytes 73736 | tf_op jit(solution)/shard_map/ppermute | solution.py:17
  181.5 9.1 %collective-permute-start.8 = (bf16[3,16,8,1]{3,0,2,1:T(4,128)(2,1)S(1)}, bf16[3,16,8,1]{3,0,2,1:T(4,128)(2,1)S(1)}, u32[]{:S(2)}, u32[]{:S(2)}) collective-permute-start(bf16[3,16,8,1]{3,0,2,1:T(4,128)(2,1)S(1)} %bitcast.89), channel_id=1, source_target_pairs={{32,0},{64,32},{96,64},{128,96},{160,128},{192,160},{224,192},{256... | collective-permute-start | bytes 2312 | tf_op jit(solution)/shard_map/ppermute | solution.py:17
  190.6 3.5 %collective-permute-start.9 = (bf16[3,16,1,129]{3,0,2,1:T(4,128)(2,1)S(1)}, bf16[3,16,1,129]{3,0,2,1:T(4,128)(2,1)S(1)}, u32[]{:S(2)}, u32[]{:S(2)}) collective-permute-start(bf16[3,16,1,129]{3,0,2,1:T(4,128)(2,1)S(1)} %fusion.214), channel_id=1, source_target_pairs={{1,0},{2,1},{3,2},{4,3},{5,4},{6,5},{7,6},{8,7},{9,8},{10,9},{11,1... | collective-permute-start | bytes 37160 | tf_op jit(solution)/shard_map/ppermute | solution.py:17
  195.8 3.1 %copy-start.1 = (s32[16,8,128]{2,1,0:T(8,128)S(1)}, s32[16,8,128]{2,1,0:T(8,128)}, u32[]{:S(2)}) copy-start(s32[16,8,128]{2,1,0:T(8,128)} %param.9) | copy-start | bytes 196612
  195.8 3.1 %copy-start.2 = (f32[16,8,128]{2,1,0:T(8,128)S(1)}, f32[16,8,128]{2,1,0:T(8,128)}, u32[]{:S(2)}) copy-start(f32[16,8,128]{2,1,0:T(8,128)} %param.8) | copy-start | bytes 196612
  195.9 3.1 %copy-start.6 = (pred[128]{0:T(512)(128)(4,1)S(1)}, pred[128]{0:T(512)(128)(4,1)}, u32[]{:S(2)}) copy-start(pred[128]{0:T(512)(128)(4,1)} %copy-done.5) | copy-start | bytes 388
  200.4 6.2 %collective-permute-start.10 = (f32[16,8,2]{2,1,0:T(8,128)S(1)}, f32[16,8,2]{2,1,0:T(8,128)S(1)}, u32[]{:S(2)}, u32[]{:S(2)}) collective-permute-start(f32[16,8,2]{2,1,0:T(8,128)S(1)} %get-tuple-element.92), channel_id=1, source_target_pairs={{0,32},{32,64},{64,96},{96,128},{128,160},{160,192},{192,224},{224... | collective-permute-start | bytes 3080 | tf_op jit(solution)/shard_map/ppermute | solution.py:25
  204.1 8.3 %collective-permute-start.11 = (f32[16,8,2]{2,1,0:T(8,128)S(1)}, f32[16,8,2]{2,1,0:T(8,128)S(1)}, u32[]{:S(2)}, u32[]{:S(2)}) collective-permute-start(f32[16,8,2]{2,1,0:T(8,128)S(1)} %get-tuple-element.93), channel_id=1, source_target_pairs={{32,0},{64,32},{96,64},{128,96},{160,128},{192,160},{224,192},{256... | collective-permute-start | bytes 3080 | tf_op jit(solution)/shard_map/ppermute | solution.py:28
  212.5 9.2 %collective-permute-start.12 = (f32[16,2,132]{2,1,0:T(2,128)S(1)}, f32[16,2,132]{2,1,0:T(2,128)S(1)}, u32[]{:S(2)}, u32[]{:S(2)}) collective-permute-start(f32[16,2,132]{2,1,0:T(2,128)S(1)} %get-tuple-element.81), channel_id=1, source_target_pairs={{0,1},{1,2},{2,3},{3,4},{4,5},{5,6},{6,7},{7,8},{8,9},{9,10},{10,1... | collective-permute-start | bytes 50696 | tf_op jit(solution)/shard_map/ppermute | solution.py:25
  214.4 8.2 %collective-permute-start.13 = (f32[16,2,132]{2,1,0:T(2,128)S(1)}, f32[16,2,132]{2,1,0:T(2,128)S(1)}, u32[]{:S(2)}, u32[]{:S(2)}) collective-permute-start(f32[16,2,132]{2,1,0:T(2,128)S(1)} %get-tuple-element.82), channel_id=1, source_target_pairs={{1,0},{2,1},{3,2},{4,3},{5,4},{6,5},{7,6},{8,7},{9,8},{10,9},{11,1... | collective-permute-start | bytes 50696 | tf_op jit(solution)/shard_map/ppermute | solution.py:28
where the time goes:
time: 228 us; the launch traced here: 225 us
  other arithmetic  69.5 us (30%)
  local copies, waits for them, and re-layouts  56.2 us (25%)
  waiting for transfers between devices  49.4 us (22%)
  starting transfers between devices  47.7 us (21%)
    scatter-add x1, other arithmetic, shards(): loads = jnp.zeros((3, depth, rows, columns), jnp.float32).at[:, load_z, j...  50.9 us
    ppermute x10, waiting for transfers between devices, passed_along(): return lax.ppermute(shard, axis, pairs)  42.5 us
    ppermute x10, starting transfers between devices, passed_along(): return lax.ppermute(shard, axis, pairs)  33.3 us
    unnamed x27, local copies, waits for them, and re-layouts  20.9 us
    another operation x3, local copies, waits for them, and re-layouts, element_terms(): jnp.stack([padded[component, depth_bit:depth_bit + depth, row_bit:row_bit...  10 us
    ppermute x2, starting transfers between devices, extended(): lax.ppermute(lax.slice_in_dim(block, 0, width, axis=dim), axis, backward)  8.88 us
    ppermute x2, waiting for transfers between devices, extended(): lax.ppermute(lax.slice_in_dim(block, 0, width, axis=dim), axis, backward)  6.65 us
    slice x8, local copies, waits for them, and re-layouts, element_terms(): padded[component, depth_bit:depth_bit + depth, row_bit:row_bit + rows, co...  5.8 us
  transfers between devices with their start and end apart: 14, of which 12 were waited for; matrix products, arithmetic and copies ran while one was open for 40% of the time, Pallas kernels for 0%

commit v1 on v0

v1 whole, which is shorter than its diff:
```python
import math

import jax
import jax.numpy as jnp
import numpy as np
from jax import lax
from jax.experimental import pallas as pl
from jax.experimental.pallas import tpu as pltpu
from jax.sharding import PartitionSpec as P

void_modulus = 0.001
spectral_mid = 1.375
spectral_half = 1.125
sigma = spectral_mid / spectral_half
first = 1.0 / sigma
second = 1.0 / (2.0 * sigma - first)

F32, BF16, I32 = jnp.float32, jnp.bfloat16, jnp.int32
DEPTH, ROWS, COLS = 16, 8, 128
LOW, HIGH = 4, 5
WIDE = 256
SPAN = LOW + HIGH
KLASS = (0, 1, 2, 4, 5, 8)


def stiffness_table():
    poisson = 0.3
    lame = poisson / ((1.0 + poisson) * (1.0 - 2.0 * poisson))
    shear = 0.5 / (1.0 + poisson)
    elastic = np.zeros((6, 6))
    elastic[:3, :3] = lame
    for index in range(3):
        elastic[index, index] += 2.0 * shear
        elastic[index + 3, index + 3] = shear
    points = [0.5 - 0.5 / math.sqrt(3.0), 0.5 + 0.5 / math.sqrt(3.0)]
    table = np.zeros((24, 24))
    for point_z in points:
        for point_y in points:
            for point_x in points:
                strain = np.zeros((6, 24))
                for corner in range(8):
                    bit_z, bit_y, bit_x = (corner // 4, corner // 2 % 2, corner % 2)
                    shape_x = point_x if bit_x else 1.0 - point_x
                    shape_y = point_y if bit_y else 1.0 - point_y
                    shape_z = point_z if bit_z else 1.0 - point_z
                    slope_x = 1.0 if bit_x else -1.0
                    slope_y = 1.0 if bit_y else -1.0
                    slope_z = 1.0 if bit_z else -1.0
                    grad_x = slope_x * shape_y * shape_z
                    grad_y = shape_x * slope_y * shape_z
                    grad_z = shape_x * shape_y * slope_z
                    strain[0, corner] = grad_x
                    strain[1, 8 + corner] = grad_y
                    strain[2, 16 + corner] = grad_z
                    strain[3, corner] = grad_y
                    strain[3, 8 + corner] = grad_x
                    strain[4, 8 + corner] = grad_z
                    strain[4, 16 + corner] = grad_y
                    strain[5, corner] = grad_z
                    strain[5, 16 + corner] = grad_x
                table += strain.T @ elastic @ strain / 8.0
    return np.asarray(table.astype(np.float32).astype(jnp.bfloat16).astype(np.float64))


def element_matrix(table):
    matrix = np.zeros((2, 2, 2, 3, DEPTH, 2, 2, 3, DEPTH))
    for corner in range(8):
        bz, by, bx = corner // 4, corner // 2 % 2, corner % 2
        for other in range(8):
            oz, oy, ox = other // 4, other // 2 % 2, other % 2
            for c in range(3):
                for k in range(3):
                    for z in range(DEPTH - 1):
                        matrix[bz, by, bx, c, z + bz, oy, ox, k, z + oz] = table[
                            c * 8 + corner, k * 8 + other
                        ]
    return matrix.reshape(384, 192)


def depth_bands():
    bands = np.zeros((6, DEPTH, 3, DEPTH))
    for z in range(DEPTH):
        for dz in range(-2, 3):
            if 0 <= z + dz < DEPTH:
                for dy in range(3):
                    bands[KLASS.index(dz * dz + dy * dy), z, dy, z + dz] = 1.0
    return bands.reshape(96, 48)


def cone(square, dx):
    return max(0.0, 3.0 - math.sqrt(square + dx * dx))


def along_bands():
    bands = np.zeros((6, WIDE, COLS))
    for k, square in enumerate(KLASS):
        for x in range(COLS):
            for dx in range(-2, 3):
                bands[k, (x + dx) % WIDE, x] = cone(square, dx)
    return bands.reshape(6 * WIDE, COLS)


def iota(shape, dim):
    return lax.broadcasted_iota(I32, shape, dim)


def starts():
    return lax.axis_index("gy") * ROWS, lax.axis_index("gx") * COLS


def call(body, outs, ins, scratch=(), flops=0, limit=None):
    whole = pl.BlockSpec(memory_space=pltpu.VMEM)
    moved = sum(math.prod(o.shape) * o.dtype.itemsize for o in outs)
    return pl.pallas_call(
        body,
        out_shape=outs,
        in_specs=[whole] * len(ins),
        out_specs=[whole] * len(outs),
        scratch_shapes=list(scratch),
        compiler_params=pltpu.CompilerParams(vmem_limit_bytes=limit or (32 << 20)),
        cost_estimate=pl.CostEstimate(flops=flops, bytes_accessed=moved, transcendentals=0),
    )(*ins)


def shape_of(shape, dtype):
    return jax.ShapeDtypeStruct(shape, dtype)


def pack_body(grid_y, grid_x, u_ref, den_ref, sol_ref, um, st_own, co_own, low, high, uf):
    y0, x0 = starts()
    uf[...] = u_ref[...].astype(F32)
    lane = iota((DEPTH, COLS), 1)
    inside_zx = (iota((DEPTH, COLS), 0) < DEPTH - 1) & (lane + x0 < grid_x - 1)
    for y in range(ROWS):
        planes = [uf[pl.ds(c * 128 + y, DEPTH, stride=ROWS), :] for c in range(3)]
        density = den_ref[pl.ds(y, DEPTH, stride=ROWS), :]
        solid = sol_ref[pl.ds(y, DEPTH, stride=ROWS), :]
        exists = inside_zx & (y0 + y < grid_y - 1)
        physical = jnp.where(solid == 1, 1.0, density)
        square = physical * physical
        stiff = jnp.where(exists, void_modulus + (1.0 - void_modulus) * (square * physical), 0.0)
        factor = jnp.where(
            exists, (-3.0 * (1.0 - void_modulus)) * square * (1 - solid).astype(F32), 0.0
        )
        st_own[y] = stiff
        co_own[y] = factor
        planes += [stiff, factor]
        below = jnp.zeros((DEPTH, COLS), F32)
        above = jnp.zeros((DEPTH, COLS), F32)
        for p, plane in enumerate(planes):
            um[y, p] = plane.astype(BF16)
            at = SPAN * p
            moved = pltpu.roll(plane, at + LOW, 1)
            above = jnp.where((lane >= at + LOW) & (lane < at + SPAN), moved, above)
            below = jnp.where((lane >= at) & (lane < at + LOW), moved, below)
        low[y] = above.astype(BF16)
        high[y] = below.astype(BF16)


def merge_body(um, right, left, up, down, merged):
    both = (right[...].astype(F32) + left[...].astype(F32)).astype(BF16)
    merged[...] = both
    for y in range(HIGH):
        up[y * 3 : y * 3 + 3] = um[y, 0:3]
    up[15:19] = um[0:4, 3]
    up[19:21] = um[0:2, 4]
    up[21:26] = both[0:HIGH]
    for y in range(LOW):
        down[y * 3 : y * 3 + 3] = um[y + 4, 0:3]
    down[12:16] = um[4:8, 3]
    down[16:18] = um[6:8, 4]
    down[18:22] = both[4:8]


def one_hot(key, rows):
    return (iota((rows, key.shape[1]), 0) == key).astype(F32).astype(BF16)


def mask_body(grid_y, grid_x, fixed, nodes, forces, free, loads, inverse, spread):
    y0, x0 = starts()

    def keys(flat):
        x = (flat & (grid_x - 1)) - x0
        y = ((flat // grid_x) & (grid_y - 1)) - y0 + LOW
        z = flat // (grid_x * grid_y)
        near = (x >= -LOW) & (x < COLS + HIGH)
        return jnp.where(near, x & (WIDE - 1), -1), y * DEPTH + z

    def dots(a, b):
        return lax.dot_general(a, b, (((1,), (1,)), ((), ())), preferred_element_type=F32)

    count = fixed.shape[1]
    part = 512
    spread[...] = jnp.zeros_like(spread)
    for at in range(0, count, part):
        kx, ky = keys(fixed[:, at : at + part])
        spread[...] += dots(one_hot(ky, 256), one_hot(kx, WIDE))
    free[...] = jnp.where(spread[...] > 0.0, 0.0, 1.0).reshape(16, DEPTH, WIDE)

    kx, ky = keys(nodes[...])
    at_x = one_hot(kx, WIDE)
    here = iota((256, kx.shape[1]), 0) == ky
    for c in range(3):
        force = forces[c : c + 1, :]
        total = jnp.zeros((256, WIDE), F32)
        for _ in range(3):
            head = force.astype(BF16).astype(F32)
            total = total + dots(jnp.where(here, head, 0.0).astype(BF16), at_x)
            force = force - head
        loads[:, c] = total.reshape(16, DEPTH, WIDE)

    lanes = iota((DEPTH, WIDE), 1)
    xpos = x0 + jnp.where(lanes < WIDE // 2 + HIGH, lanes, lanes - WIDE)

    def within(pos, size):
        return jnp.where((pos >= 0) & (pos < size - 1), 1.0, 0.0)

    ex = [within(xpos + d, grid_x) for d in range(-2, 3)]
    rows_of = {
        k: sum(cone(k, d) * ex[d + 2] for d in range(-2, 3) if cone(k, d) > 0.0) for k in KLASS
    }
    zpos = iota((DEPTH, WIDE), 0)
    ez = [within(zpos + d, DEPTH) for d in range(-2, 3)]
    z_terms = (ez[2], ez[1] + ez[3], ez[0] + ez[4])
    for row in range(12):
        ypos = y0 + row - 2
        ey = [within(ypos + d, grid_y) for d in range(-2, 3)]
        y_terms = (ey[2], ey[1] + ey[3], ey[0] + ey[4])
        total = jnp.zeros((DEPTH, WIDE), F32)
        for a in range(3):
            inner = sum(y_terms[b] * rows_of[a * a + b * b] for b in range(3))
            total = total + z_terms[a] * inner
        alive = ez[2] * ex[2] * ey[2] > 0.0
        inverse[row] = jnp.where(alive, 1.0 / jnp.where(alive, total, 1.0), 0.0)


def main_body(
    pivot,
    um,
    st_own,
    co_own,
    merged,
    up,
    down,
    free,
    loads,
    inverse,
    matrix,
    bands_z,
    bands_x,
    smoothed,
    filtered,
    uu,
    ss,
    vv,
    st,
    st1,
    co,
    res,
    inv,
    ratio,
    layers,
    out_f,
):
    lane = iota((DEPTH, COLS), 1)
    edge = (lane < HIGH) | (lane >= COLS - LOW)

    def rim(packed, p):
        return jnp.where(edge, pltpu.roll(packed, COLS - SPAN * p - LOW, 1), 0.0)

    def put(ref, row, fields):
        ref[pl.ds(row * 96, 48), :] = fields.astype(BF16)
        ref[pl.ds(row * 96 + 48, 48), :] = pltpu.roll(fields, WIDE - 1, 1).astype(BF16)

    for row in range(17):
        n = row - LOW
        if n < 0:
            tiles = [down[row * 3 + c].astype(F32) for c in range(3)]
            packed = down[18 + row].astype(F32)
            stiff = down[12 + row].astype(F32)
            factor = down[16 + row - 2].astype(F32) if n >= -2 else None
        elif n < ROWS:
            tiles = [um[n, c].astype(F32) for c in range(3)]
            packed = merged[n].astype(F32)
            stiff, factor = st_own[n], co_own[n]
        else:
            m = n - ROWS
            tiles = [up[m * 3 + c].astype(F32) for c in range(3)]
            packed = up[21 + m].astype(F32)
            stiff = up[15 + m].astype(F32) if m < 4 else None
            factor = up[19 + m].astype(F32) if m < 2 else None
        fields = jnp.concatenate(
            [jnp.concatenate([tiles[c], rim(packed, c)], axis=1) for c in range(3)], axis=0
        )
        put(uu, row, fields)
        if stiff is not None:
            value = jnp.concatenate([stiff, rim(packed, 3)], axis=1)
            st[row] = value
            st1[row] = pltpu.roll(value, 1, 0)
        if factor is not None:
            co[row - 2] = jnp.concatenate([factor, rim(packed, 4)], axis=1)

    def forces(ref, row, carry):
        x = ref[pl.ds(row * 96, 192), :]
        f = jnp.dot(matrix[...], x, preferred_element_type=F32).reshape(2, 12, DEPTH, WIDE)
        g = (f[0] * st[row][None] + f[1] * st1[row][None]).reshape(2, 2, 3 * DEPTH, WIDE)
        h = g[0] + carry
        return h[0] + pltpu.roll(h[1], 1, 1), g[1]

    def first_step(row, carry):
        before, weight = carry
        applied, after = forces(uu, row, before)
        here = st[row] + st1[row]
        both = here + weight
        diagonal = pivot * (both + pltpu.roll(both, 1, 1))
        some = diagonal > 0.0
        inverse_diagonal = jnp.where(some, 1.0 / jnp.where(some, diagonal, 1.0), 0.0)
        inv[row] = inverse_diagonal
        mask = free[row]
        residual = (loads[row] - applied.reshape(3, DEPTH, WIDE)) * mask[None]
        res[row] = residual
        step = (residual * (inverse_diagonal * (1.0 / spectral_mid))[None]).astype(BF16)
        put(ss, row, step.astype(F32).reshape(48, WIDE))
        return after, here

    zero = jnp.zeros((2, 48, WIDE), F32)
    lax.fori_loop(0, 16, first_step, (zero, jnp.zeros((DEPTH, WIDE), F32)))

    def second_step(row, carry):
        applied, after = forces(ss, row, carry)
        step0 = ss[pl.ds(row * 96, 48), :].astype(F32).reshape(3, DEPTH, WIDE)
        old = uu[pl.ds(row * 96, 48), :].astype(F32).reshape(3, DEPTH, WIDE)
        residual = res[row] - applied.reshape(3, DEPTH, WIDE) * free[row][None]
        step1 = (second * first) * step0 + residual * (
            (2.0 * second / spectral_half) * inv[row]
        )[None]
        new = (old + step0 + step1).astype(BF16).astype(F32)
        put(vv, row, new.reshape(48, WIDE))
        return after

    lax.fori_loop(1, 15, second_step, zero)

    for y in range(ROWS):
        for c in range(3):
            out_f[pl.ds(c * 128 + y, DEPTH, stride=ROWS), :] = vv[
                (y + LOW) * 96 + c * 16 : (y + LOW) * 96 + c * 16 + 16, 0:COLS
            ].astype(F32)
    smoothed[...] = out_f[...].astype(BF16)

    def energy_step(row, carry):
        x = vv[pl.ds(row * 96, 192), :]
        f = jnp.dot(matrix[...], x, preferred_element_type=F32).reshape(2, 12, DEPTH, WIDE)
        u = x.astype(F32).reshape(12, DEPTH, WIDE)
        here = jnp.sum(f[0] * u, axis=0)
        over = jnp.sum(f[1] * u, axis=0)
        energy = here + pltpu.roll(over, DEPTH - 1, 0)
        ratio[row - 2] = energy * co[row - 2] * inverse[row - 2]
        return carry

    lax.fori_loop(2, 14, energy_step, 0)

    for y in range(ROWS):
        a = jnp.concatenate(
            [ratio[y + 2], ratio[y + 1] + ratio[y + 3], ratio[y] + ratio[y + 4]], axis=0
        )
        s = jnp.dot(bands_z[...], a.astype(BF16), preferred_element_type=F32).astype(BF16)
        for k in range(6):
            layers[y * DEPTH : (y + 1) * DEPTH, k * WIDE : (k + 1) * WIDE] = s[
                k * DEPTH : (k + 1) * DEPTH
            ]
    total = jnp.dot(layers[...], bands_x[...], preferred_element_type=F32)
    for y in range(ROWS):
        keep = jnp.where(co_own[y] < 0.0, total[y * DEPTH : (y + 1) * DEPTH], 0.0)
        filtered[pl.ds(y, DEPTH, stride=ROWS), :] = keep


def passed_along(shard, axis, by):
    size = lax.axis_size(axis)
    return lax.ppermute(shard, axis, [(i, i + by) for i in range(size) if 0 <= i + by < size])


def shards(displacement, density, solid, fixed_nodes, load_nodes, load_forces):
    grid_y = ROWS * lax.axis_size("gy")
    grid_x = COLS * lax.axis_size("gx")
    table = stiffness_table()
    pivot = float(table[0, 0])
    tile = (DEPTH, COLS)

    um, st_own, co_own, low, high = call(
        lambda *refs: pack_body(grid_y, grid_x, *refs),
        [
            shape_of((ROWS, 5) + tile, BF16),
            shape_of((ROWS,) + tile, F32),
            shape_of((ROWS,) + tile, F32),
            shape_of((ROWS,) + tile, BF16),
            shape_of((ROWS,) + tile, BF16),
        ],
        [displacement.reshape(384, 128), density.reshape(128, 128), solid.reshape(128, 128)],
        [pltpu.VMEM((384, 128), F32)],
    )
    right = passed_along(low, "gx", -1)
    left = passed_along(high, "gx", 1)
    free, loads, inverse = call(
        lambda *refs: mask_body(grid_y, grid_x, *refs),
        [
            shape_of((16, DEPTH, WIDE), F32),
            shape_of((16, 3, DEPTH, WIDE), F32),
            shape_of((12, DEPTH, WIDE), F32),
        ],
        [fixed_nodes.reshape(1, -1), load_nodes.reshape(1, -1), load_forces.T],
        [pltpu.VMEM((256, WIDE), F32)],
        flops=2000000000,
    )
    up, down, merged = call(
        merge_body,
        [
            shape_of((26,) + tile, BF16),
            shape_of((22,) + tile, BF16),
            shape_of((ROWS,) + tile, BF16),
        ],
        [um, right, left],
    )
    from_above = passed_along(up, "gy", -1)
    from_below = passed_along(down, "gy", 1)
    smoothed, filtered = call(
        lambda *refs: main_body(pivot, *refs),
        [shape_of((384, 128), BF16), shape_of((128, 128), F32)],
        [
            um,
            st_own,
            co_own,
            merged,
            from_above,
            from_below,
            free,
            loads,
            inverse,
            jnp.asarray(element_matrix(table), BF16),
            jnp.asarray(depth_bands(), BF16),
            jnp.asarray(along_bands(), BF16),
        ],
        [
            pltpu.VMEM((17 * 96, WIDE), BF16),
            pltpu.VMEM((16 * 96, WIDE), BF16),
            pltpu.VMEM((15 * 96, WIDE), BF16),
            pltpu.VMEM((16, DEPTH, WIDE), F32),
            pltpu.VMEM((16, DEPTH, WIDE), F32),
            pltpu.VMEM((12, DEPTH, WIDE), F32),
            pltpu.VMEM((16, 3, DEPTH, WIDE), F32),
            pltpu.VMEM((16, DEPTH, WIDE), F32),
            pltpu.VMEM((12, DEPTH, WIDE), F32),
            pltpu.VMEM((128, 6 * WIDE), BF16),
            pltpu.VMEM((384, 128), F32),
        ],
        flops=10000000000,
    )
    return smoothed.reshape(3, DEPTH, ROWS, COLS), filtered.reshape(DEPTH, ROWS, COLS)


def solution(mesh):
    placed = (P(None, None, "gy", "gx"), P(None, "gy", "gx"), P(None, "gy", "gx"), P(), P(), P())
    return jax.shard_map(
        shards,
        mesh=mesh,
        in_specs=placed,
        out_specs=(P(None, None, "gy", "gx"), P(None, "gy", "gx")),
        check_vma=False,
    )
```

time: 228 us -> 46.2 us (0.20)
  the two profiles are of different devices: /device:TPU:60 before, /device:TPU:199 now
where the time goes in v1:
time: 46.2 us; the launch traced here: 45.9 us
  starting transfers between devices  17 us (37%)
  Pallas kernels  16 us (35%)
  waiting for transfers between devices  9.45 us (20%)
  local copies, waits for them, and re-layouts  2.6 us (6%)
  between operations  0.76 us (2%)
    ppermute x4, starting transfers between devices, passed_along(): lax.ppermute(shard, axis, [(i, i + by) for i in range(size) if 0 <= i + b...  17 us
    pallas_call x4, Pallas kernels, call(): pl.pallas_call(body, out_shape=outs, in_specs=[whole] * len(ins), out_spe...  16 us
    ppermute x4, waiting for transfers between devices, passed_along(): lax.ppermute(shard, axis, [(i, i + by) for i in range(size) if 0 <= i + b...  9.45 us
    unnamed x18, local copies, waits for them, and re-layouts  2.6 us
  transfers between devices with their start and end apart: 4, of which 2 were waited for; matrix products, arithmetic and copies ran while one was open for 0% of the time, Pallas kernels for 3%

profile of v1, /device:TPU:199, one launch (start us, length us, event | category | flops | bytes accessed | tf_op | source)
XLA Modules:
  0.0 45.9 jit_solution(713404933810782692)
XLA Ops:
  0.6 0.0 copy-start
  0.6 0.9 %copy-done = bf16[3,16,8,128]{3,2,1,0:T(8,128)(2,1)S(1)} copy-done((bf16[3,16,8,128]{3,2,1,0:T(8,128)(2,1)S(1)}, bf16[3,16,8,128]{3,2,1,0:T(8,128)(2,1)}, u32[]{:S(2)}) %copy-start) | copy-done | bytes 98328
  1.5 0.8 %copy-done.1 = f32[16,8,128]{2,1,0:T(8,128)S(1)} copy-done((f32[16,8,128]{2,1,0:T(8,128)S(1)}, f32[16,8,128]{2,1,0:T(8,128)}, u32[]{:S(2)}) %copy-start.1) | copy-done | bytes 65560
  2.4 0.8 %copy-done.2 = s32[16,8,128]{2,1,0:T(8,128)S(1)} copy-done((s32[16,8,128]{2,1,0:T(8,128)S(1)}, s32[16,8,128]{2,1,0:T(8,128)}, u32[]{:S(2)}) %copy-start.2) | copy-done | bytes 65560
  3.2 0.2 shard_map.104
  3.4 4.2 %collective-permute-start = (bf16[8,16,128]{2,1,0:T(8,128)(2,1)S(1)}, bf16[8,16,128]{2,1,0:T(8,128)(2,1)S(1)}, u32[]{:S(2)}, u32[]{:S(2)}) collective-permute-start(bf16[8,16,128]{2,1,0:T(8,128)(2,1)S(1)} %get-tuple-element.18), channel_id=1, source_target_pairs={{32,0},{64,32},{96,64},{128,96},{160,128},{192,160},{224,192},{256... | collective-permute-start | bytes 98312 | tf_op jit(solution)/shard_map/ppermute | solution.py:379
  7.6 1.9 %collective-permute-start.1 = (bf16[8,16,128]{2,1,0:T(8,128)(2,1)S(1)}, bf16[8,16,128]{2,1,0:T(8,128)(2,1)S(1)}, u32[]{:S(2)}, u32[]{:S(2)}) collective-permute-start(bf16[8,16,128]{2,1,0:T(8,128)(2,1)S(1)} %get-tuple-element.19), channel_id=1, source_target_pairs={{0,32},{32,64},{64,96},{96,128},{128,160},{160,192},{192,224},{224... | collective-permute-start | bytes 98312 | tf_op jit(solution)/shard_map/ppermute | solution.py:379
  9.5 0.0 collective-permute-done.right
  9.5 4.8 %collective-permute-done.1.left = bf16[8,16,128]{2,1,0:T(8,128)(2,1)S(1)} collective-permute-done((bf16[8,16,128]{2,1,0:T(8,128)(2,1)S(1)}, bf16[8,16,128]{2,1,0:T(8,128)(2,1)S(1)}, u32[]{:S(2)}, u32[]{:S(2)}) %collective-permute-start.1) | collective-permute-done | bytes 32800 | tf_op jit(solution)/shard_map/ppermute | solution.py:379
  14.4 0.0 copy-start.4
  14.4 9.0 %collective-permute-start.3 = (bf16[22,16,128]{2,1,0:T(8,128)(2,1)S(1)}, bf16[22,16,128]{2,1,0:T(8,128)(2,1)S(1)}, u32[]{:S(2)}, u32[]{:S(2)}) collective-permute-start(bf16[22,16,128]{2,1,0:T(8,128)(2,1)S(1)} %get-tuple-element.22), channel_id=1, source_target_pairs={{0,1},{1,2},{2,3},{3,4},{4,5},{5,6},{6,7},{7,8},{8,9},{9,10},{10,1... | collective-permute-start | bytes 270344 | tf_op jit(solution)/shard_map/ppermute | solution.py:379
  23.4 1.9 %collective-permute-start.2 = (bf16[26,16,128]{2,1,0:T(8,128)(2,1)S(1)}, bf16[26,16,128]{2,1,0:T(8,128)(2,1)S(1)}, u32[]{:S(2)}, u32[]{:S(2)}) collective-permute-start(bf16[26,16,128]{2,1,0:T(8,128)(2,1)S(1)} %get-tuple-element.21), channel_id=1, source_target_pairs={{1,0},{2,1},{3,2},{4,3},{5,4},{6,5},{7,6},{8,7},{9,8},{10,9},{11,1... | collective-permute-start | bytes 319496 | tf_op jit(solution)/shard_map/ppermute | solution.py:379
  25.3 0.0 copy-done.3
  25.3 0.0 copy-done.5
  25.3 0.0 copy-done.4
  25.4 0.0 copy-start.6
  25.4 0.0 copy-start.7
  25.4 0.0 copy-start.8
  25.4 1.5 %shard_map.106 = (f32[16,16,256]{2,1,0:T(8,128)S(1)}, f32[16,3,16,256]{3,2,1,0:T(8,128)S(1)}, f32[12,16,256]{2,1,0:T(8,128)S(1)}) custom-call(s32[1,4096]{1,0:T(1,128)S(1)} %bitcast.11, s32[1,512]{1,0:T(1,128)S(1)} %bitcast.13, f32[3,512]{1,0:T(4,128)S(1)} %bitcast.12), custom_call_target="tpu_custom_call" | custom-call | flops 2000000000 | bytes 1245184 | tf_op jit(solution)/shard_map/pallas_call | solution.py:114
  26.9 0.0 collective-permute-done.3.refs_5_
  26.9 4.6 %collective-permute-done.2.refs_4_ = bf16[26,16,128]{2,1,0:T(8,128)(2,1)S(1)} collective-permute-done((bf16[26,16,128]{2,1,0:T(8,128)(2,1)S(1)}, bf16[26,16,128]{2,1,0:T(8,128)(2,1)S(1)}, u32[]{:S(2)}, u32[]{:S(2)}) %collective-permute-start.2) | collective-permute-done | bytes 106528 | tf_op jit(solution)/shard_map/ppermute | solution.py:379
  31.5 0.0 copy-done.6
  31.5 0.0 copy-done.8
  31.5 14.3 %shard_map.107 = (bf16[384,128]{1,0:T(8,128)(2,1)}, f32[128,128]{1,0:T(8,128)}) custom-call(bf16[8,5,16,128]{3,2,1,0:T(8,128)(2,1)S(1)} %get-tuple-element.15.um.refs_0_, f32[8,16,128]{2,1,0:T(8,128)S(1)} %get-tuple-element.16.refs_1_, f32[8,16,128]{2,1,0:T(8,128)S(1)} %get-tuple-element.17.refs_2_, bf16[8,16,128]{2,1,0:T(8,128)(2,1)S(1)} %get-tuple-element.20.refs_3_, ...), custom_call_target="tpu_custom_call" | custom-call | flops 10000000000 | bytes 163840 | tf_op jit(solution)/shard_map/pallas_call | solution.py:114
  (6 shorter events, 0.0 us)
Async XLA Ops:
  0.6 0.9 %copy-start = (bf16[3,16,8,128]{3,2,1,0:T(8,128)(2,1)S(1)}, bf16[3,16,8,128]{3,2,1,0:T(8,128)(2,1)}, u32[]{:S(2)}) copy-start(bf16[3,16,8,128]{3,2,1,0:T(8,128)(2,1)} %param.9) | copy-start | bytes 294916
  1.5 0.8 %copy-start.1 = (f32[16,8,128]{2,1,0:T(8,128)S(1)}, f32[16,8,128]{2,1,0:T(8,128)}, u32[]{:S(2)}) copy-start(f32[16,8,128]{2,1,0:T(8,128)} %param.10) | copy-start | bytes 196612
  2.4 0.8 %copy-start.2 = (s32[16,8,128]{2,1,0:T(8,128)S(1)}, s32[16,8,128]{2,1,0:T(8,128)}, u32[]{:S(2)}) copy-start(s32[16,8,128]{2,1,0:T(8,128)} %param.11) | copy-start | bytes 196612
  3.4 6.1 %collective-permute-start = (bf16[8,16,128]{2,1,0:T(8,128)(2,1)S(1)}, bf16[8,16,128]{2,1,0:T(8,128)(2,1)S(1)}, u32[]{:S(2)}, u32[]{:S(2)}) collective-permute-start(bf16[8,16,128]{2,1,0:T(8,128)(2,1)S(1)} %get-tuple-element.18), channel_id=1, source_target_pairs={{32,0},{64,32},{96,64},{128,96},{160,128},{192,160},{224,192},{256... | collective-permute-start | bytes 98312 | tf_op jit(solution)/shard_map/ppermute | solution.py:379
  7.6 6.8 %collective-permute-start.1 = (bf16[8,16,128]{2,1,0:T(8,128)(2,1)S(1)}, bf16[8,16,128]{2,1,0:T(8,128)(2,1)S(1)}, u32[]{:S(2)}, u32[]{:S(2)}) collective-permute-start(bf16[8,16,128]{2,1,0:T(8,128)(2,1)S(1)} %get-tuple-element.19), channel_id=1, source_target_pairs={{0,32},{32,64},{64,96},{96,128},{128,160},{160,192},{192,224},{224... | collective-permute-start | bytes 98312 | tf_op jit(solution)/shard_map/ppermute | solution.py:379
  14.3 11.0 %copy-start.3 = (s32[4096]{0:T(1024)S(1)}, s32[4096]{0:T(1024)}, u32[]{:S(2)}) copy-start(s32[4096]{0:T(1024)} %param.12) | copy-start | bytes 49156
  14.3 11.0 %copy-start.5 = (s32[512]{0:T(512)S(1)}, s32[512]{0:T(512)}, u32[]{:S(2)}) copy-start(s32[512]{0:T(512)} %param.13) | copy-start | bytes 6148
  14.4 11.0 %copy-start.4 = (f32[512,3]{0,1:T(4,128)S(1)}, f32[512,3]{0,1:T(4,128)}, u32[]{:S(2)}) copy-start(f32[512,3]{0,1:T(4,128)} %param.14) | copy-start | bytes 18436
  14.4 12.5 %collective-permute-start.3 = (bf16[22,16,128]{2,1,0:T(8,128)(2,1)S(1)}, bf16[22,16,128]{2,1,0:T(8,128)(2,1)S(1)}, u32[]{:S(2)}, u32[]{:S(2)}) collective-permute-start(bf16[22,16,128]{2,1,0:T(8,128)(2,1)S(1)} %get-tuple-element.22), channel_id=1, source_target_pairs={{0,1},{1,2},{2,3},{3,4},{4,5},{5,6},{6,7},{7,8},{8,9},{9,10},{10,1... | collective-permute-start | bytes 270344 | tf_op jit(solution)/shard_map/ppermute | solution.py:379
  23.4 8.1 %collective-permute-start.2 = (bf16[26,16,128]{2,1,0:T(8,128)(2,1)S(1)}, bf16[26,16,128]{2,1,0:T(8,128)(2,1)S(1)}, u32[]{:S(2)}, u32[]{:S(2)}) collective-permute-start(bf16[26,16,128]{2,1,0:T(8,128)(2,1)S(1)} %get-tuple-element.21), channel_id=1, source_target_pairs={{1,0},{2,1},{3,2},{4,3},{5,4},{6,5},{7,6},{8,7},{9,8},{10,9},{11,1... | collective-permute-start | bytes 319496 | tf_op jit(solution)/shard_map/ppermute | solution.py:379
  25.4 6.2 %copy-start.6 = (bf16[1536,128]{1,0:T(8,128)(2,1)S(1)}, bf16[1536,128]{1,0:T(8,128)(2,1)}, u32[]{:S(2)}) copy-start(bf16[1536,128]{1,0:T(8,128)(2,1)} %constant.8.clone.refs_11_) | copy-start | bytes 1179652
  25.4 6.2 %copy-start.7 = (bf16[384,192]{1,0:T(8,128)(2,1)S(1)}, bf16[384,192]{1,0:T(8,128)(2,1)}, u32[]{:S(2)}) copy-start(bf16[384,192]{1,0:T(8,128)(2,1)} %constant.6.clone.refs_9_) | copy-start | bytes 442372
  25.4 6.2 %copy-start.8 = (bf16[96,48]{1,0:T(8,128)(2,1)S(1)}, bf16[96,48]{1,0:T(8,128)(2,1)}, u32[]{:S(2)}) copy-start(bf16[96,48]{1,0:T(8,128)(2,1)} %constant.7.clone.refs_10_) | copy-start | bytes 27652

commit v2 on v1

--- a/solution.py
+++ b/solution.py
@@ -108,13 +108,13 @@
     return lax.axis_index("gy") * ROWS, lax.axis_index("gx") * COLS
 
 
-def call(body, outs, ins, scratch=(), flops=0, limit=None):
+def call(body, outs, ins, scratch=(), flops=0, limit=None, space=pltpu.VMEM):
     whole = pl.BlockSpec(memory_space=pltpu.VMEM)
     moved = sum(math.prod(o.shape) * o.dtype.itemsize for o in outs)
     return pl.pallas_call(
         body,
         out_shape=outs,
-        in_specs=[whole] * len(ins),
+        in_specs=[pl.BlockSpec(memory_space=space)] * len(ins),
         out_specs=[whole] * len(outs),
         scratch_shapes=list(scratch),
         compiler_params=pltpu.CompilerParams(vmem_limit_bytes=limit or (32 << 20)),
@@ -126,8 +126,21 @@
     return jax.ShapeDtypeStruct(shape, dtype)
 
 
-def pack_body(grid_y, grid_x, u_ref, den_ref, sol_ref, um, st_own, co_own, low, high, uf):
+def pack_body(
+    grid_y, grid_x, u_in, den_in, sol_in, um, st_own, co_own, far, near, u_ref, den_ref, sol_ref, uf, sem
+):
+    copies = [
+        pltpu.make_async_copy(source, target, sem.at[i])
+        for i, (source, target) in enumerate(
+            ((u_in, u_ref), (den_in, den_ref), (sol_in, sol_ref))
+        )
+    ]
+    for copy in copies:
+        copy.start()
     y0, x0 = starts()
+    odd = lax.axis_index("gx") % 2 == 1
+    for copy in copies:
+        copy.wait()
     uf[...] = u_ref[...].astype(F32)
     lane = iota((DEPTH, COLS), 1)
     inside_zx = (iota((DEPTH, COLS), 0) < DEPTH - 1) & (lane + x0 < grid_x - 1)
@@ -153,23 +166,30 @@
             moved = pltpu.roll(plane, at + LOW, 1)
             above = jnp.where((lane >= at + LOW) & (lane < at + SPAN), moved, above)
             below = jnp.where((lane >= at) & (lane < at + LOW), moved, below)
-        low[y] = above.astype(BF16)
-        high[y] = below.astype(BF16)
-
-
-def merge_body(um, right, left, up, down, merged):
-    both = (right[...].astype(F32) + left[...].astype(F32)).astype(BF16)
+        far[y] = jnp.where(odd, below, above).astype(BF16)
+        near[y] = jnp.where(odd, above, below).astype(BF16)
+
+
+def merge_body(um, from_far, from_near, far, near, merged):
+    both = (from_far[...].astype(F32) + from_near[...].astype(F32)).astype(BF16)
     merged[...] = both
-    for y in range(HIGH):
-        up[y * 3 : y * 3 + 3] = um[y, 0:3]
-    up[15:19] = um[0:4, 3]
-    up[19:21] = um[0:2, 4]
-    up[21:26] = both[0:HIGH]
-    for y in range(LOW):
-        down[y * 3 : y * 3 + 3] = um[y + 4, 0:3]
-    down[12:16] = um[4:8, 3]
-    down[16:18] = um[6:8, 4]
-    down[18:22] = both[4:8]
+
+    def fill(up, down):
+        for y in range(HIGH):
+            up[y * 3 : y * 3 + 3] = um[y, 0:3]
+        up[15:19] = um[0:4, 3]
+        up[19:21] = um[0:2, 4]
+        up[21:26] = both[0:HIGH]
+        for y in range(LOW):
+            down[y * 3 : y * 3 + 3] = um[y + 4, 0:3]
+        down[12:16] = um[4:8, 3]
+        down[16:18] = um[6:8, 4]
+        down[18:22] = both[4:8]
+        down[22:26] = jnp.zeros((4, DEPTH, COLS), BF16)
+
+    odd = lax.axis_index("gy") % 2 == 1
+    pl.when(odd)(lambda: fill(near, far))
+    pl.when(jnp.logical_not(odd))(lambda: fill(far, near))
 
 
 def one_hot(key, rows):
@@ -240,8 +260,8 @@
     st_own,
     co_own,
     merged,
-    up,
-    down,
+    from_far,
+    from_near,
     free,
     loads,
     inverse,
@@ -262,7 +282,15 @@
     layers,
     out_f,
 ):
+    odd = lax.axis_index("gy") % 2 == 1
     lane = iota((DEPTH, COLS), 1)
+
+    def above(i):
+        return jnp.where(odd, from_far[i].astype(F32), from_near[i].astype(F32))
+
+    def below(i):
+        return jnp.where(odd, from_near[i].astype(F32), from_far[i].astype(F32))
+
     edge = (lane < HIGH) | (lane >= COLS - LOW)
 
     def rim(packed, p):
@@ -275,20 +303,20 @@
     for row in range(17):
         n = row - LOW
         if n < 0:
-            tiles = [down[row * 3 + c].astype(F32) for c in range(3)]
-            packed = down[18 + row].astype(F32)
-            stiff = down[12 + row].astype(F32)
-            factor = down[16 + row - 2].astype(F32) if n >= -2 else None
+            tiles = [below(row * 3 + c) for c in range(3)]
+            packed = below(18 + row)
+            stiff = below(12 + row)
+            factor = below(16 + row - 2) if n >= -2 else None
         elif n < ROWS:
             tiles = [um[n, c].astype(F32) for c in range(3)]
             packed = merged[n].astype(F32)
             stiff, factor = st_own[n], co_own[n]
         else:
             m = n - ROWS
-            tiles = [up[m * 3 + c].astype(F32) for c in range(3)]
-            packed = up[21 + m].astype(F32)
-            stiff = up[15 + m].astype(F32) if m < 4 else None
-            factor = up[19 + m].astype(F32) if m < 2 else None
+            tiles = [above(m * 3 + c) for c in range(3)]
+            packed = above(21 + m)
+            stiff = above(15 + m) if m < 4 else None
+            factor = above(19 + m) if m < 2 else None
         fields = jnp.concatenate(
             [jnp.concatenate([tiles[c], rim(packed, c)], axis=1) for c in range(3)], axis=0
         )
@@ -324,7 +352,7 @@
         return after, here
 
     zero = jnp.zeros((2, 48, WIDE), F32)
-    lax.fori_loop(0, 16, first_step, (zero, jnp.zeros((DEPTH, WIDE), F32)))
+    lax.fori_loop(0, 16, first_step, (zero, jnp.zeros((DEPTH, WIDE), F32)), unroll=4)
 
     def second_step(row, carry):
         applied, after = forces(ss, row, carry)
@@ -338,7 +366,7 @@
         put(vv, row, new.reshape(48, WIDE))
         return after
 
-    lax.fori_loop(1, 15, second_step, zero)
+    lax.fori_loop(1, 15, second_step, zero, unroll=4)
 
     for y in range(ROWS):
         for c in range(3):
@@ -357,7 +385,7 @@
         ratio[row - 2] = energy * co[row - 2] * inverse[row - 2]
         return carry
 
-    lax.fori_loop(2, 14, energy_step, 0)
+    lax.fori_loop(2, 14, energy_step, 0, unroll=4)
 
     for y in range(ROWS):
         a = jnp.concatenate(
@@ -374,9 +402,10 @@
         filtered[pl.ds(y, DEPTH, stride=ROWS), :] = keep
 
 
-def passed_along(shard, axis, by):
+def swapped(shard, axis, odd):
     size = lax.axis_size(axis)
-    return lax.ppermute(shard, axis, [(i, i + by) for i in range(size) if 0 <= i + by < size])
+    partner = [((i - odd) ^ 1) + odd for i in range(size)]
+    return lax.ppermute(shard, axis, [(i, j) for i, j in enumerate(partner) if 0 <= j < size])
 
 
 def shards(displacement, density, solid, fixed_nodes, load_nodes, load_forces):
@@ -386,7 +415,7 @@
     pivot = float(table[0, 0])
     tile = (DEPTH, COLS)
 
-    um, st_own, co_own, low, high = call(
+    um, st_own, co_own, far, near = call(
         lambda *refs: pack_body(grid_y, grid_x, *refs),
         [
             shape_of((ROWS, 5) + tile, BF16),
@@ -395,11 +424,22 @@
             shape_of((ROWS,) + tile, BF16),
             shape_of((ROWS,) + tile, BF16),
         ],
-        [displacement.reshape(384, 128), density.reshape(128, 128), solid.reshape(128, 128)],
-        [pltpu.VMEM((384, 128), F32)],
+        [
+            pltpu.with_memory_space_constraint(a, pltpu.HBM)
+            for a in (displacement.reshape(384, 128), density.reshape(128, 128), solid.reshape(128, 128))
+        ],
+        [
+            pltpu.VMEM((384, 128), BF16),
+            pltpu.VMEM((128, 128), F32),
+            pltpu.VMEM((128, 128), I32),
+            pltpu.VMEM((384, 128), F32),
+            pltpu.SemaphoreType.DMA((3,)),
+        ],
+        space=pltpu.HBM,
     )
-    right = passed_along(low, "gx", -1)
-    left = passed_along(high, "gx", 1)
+    nodes, _ = lax.optimization_barrier((fixed_nodes, far))
+    from_far = swapped(far, "gx", 1)
+    from_near = swapped(near, "gx", 0)
     free, loads, inverse = call(
         lambda *refs: mask_body(grid_y, grid_x, *refs),
         [
@@ -407,21 +447,22 @@
             shape_of((16, 3, DEPTH, WIDE), F32),
             shape_of((12, DEPTH, WIDE), F32),
         ],
-        [fixed_nodes.reshape(1, -1), load_nodes.reshape(1, -1), load_forces.T],
+        [nodes.reshape(1, -1), load_nodes.reshape(1, -1), load_forces.T],
         [pltpu.VMEM((256, WIDE), F32)],
         flops=2000000000,
     )
-    up, down, merged = call(
+    from_far, from_near, free = lax.optimization_barrier((from_far, from_near, free))
+    far, near, merged = call(
         merge_body,
         [
             shape_of((26,) + tile, BF16),
-            shape_of((22,) + tile, BF16),
+            shape_of((26,) + tile, BF16),
             shape_of((ROWS,) + tile, BF16),
         ],
-        [um, right, left],
+        [um, from_far, from_near],
     )
-    from_above = passed_along(up, "gy", -1)
-    from_below = passed_along(down, "gy", 1)
+    from_far = swapped(far, "gy", 1)
+    from_near = swapped(near, "gy", 0)
     smoothed, filtered = call(
         lambda *refs: main_body(pivot, *refs),
         [shape_of((384, 128), BF16), shape_of((128, 128), F32)],
@@ -430,8 +471,8 @@
             st_own,
             co_own,
             merged,
-            from_above,
-            from_below,
+            from_far,
+            from_near,
             free,
             loads,
             inverse,

time: 46.2 us -> 33.4 us (0.72)
  the two profiles are of different devices: /device:TPU:199 before, /device:TPU:63 now
where the time goes in v2:
time: 33.4 us; the launch traced here: 33.2 us
  starting transfers between devices  19.6 us (59%)
  Pallas kernels  10 us (30%)
  waiting for transfers between devices  2.68 us (8%)
  between operations  0.77 us (2%)
    ppermute x4, starting transfers between devices, swapped(): lax.ppermute(shard, axis, [(i, j) for i, j in enumerate(partner) if 0 <=...  19.6 us
    pallas_call x4, Pallas kernels, call(): pl.pallas_call(body, out_shape=outs, in_specs=[pl.BlockSpec(memory_space=...  10 us
    ppermute x4, waiting for transfers between devices, swapped(): lax.ppermute(shard, axis, [(i, j) for i, j in enumerate(partner) if 0 <=...  2.68 us
  transfers between devices with their start and end apart: 4, of which 2 were waited for; matrix products, arithmetic and copies ran while one was open for 0% of the time, Pallas kernels for 5%

profile of v2, /device:TPU:63, one launch (start us, length us, event | category | flops | bytes accessed | tf_op | source)
XLA Modules:
  0.0 33.2 jit_solution(5139415457595880586)
XLA Ops:
  0.6 0.0 copy-start
  0.6 0.0 copy-start.2
  0.7 1.1 %shard_map.104 = (bf16[8,5,16,128]{3,2,1,0:T(8,128)(2,1)S(1)}, f32[8,16,128]{2,1,0:T(8,128)S(1)}, f32[8,16,128]{2,1,0:T(8,128)S(1)}, bf16[8,16,128]{2,1,0:T(8,128)(2,1)S(1)}, bf16[8,16,128]{2,1,0:T(8,128)(2,1)S(1)}) custom-call(bf16[384,128]{1,0:T(8,128)(2,1)} %bitcast.11, f32[128,128]{1,0:T(8,128)} %bitcast.12, s32[128,128]{1,0:T(8,128)} %bitcast.13), custom_call_target="tpu_custom_call" | custom-call | bytes 360448 | tf_op jit(solution)/shard_map/pallas_call | solution.py:114
  1.8 0.0 copy-start.1
  1.8 3.0 %collective-permute-start.1 = (bf16[8,16,128]{2,1,0:T(8,128)(2,1)S(1)}, bf16[8,16,128]{2,1,0:T(8,128)(2,1)S(1)}, u32[]{:S(2)}, u32[]{:S(2)}) collective-permute-start(bf16[8,16,128]{2,1,0:T(8,128)(2,1)S(1)} %get-tuple-element.23), channel_id=1, source_target_pairs={{0,32},{32,0},{64,96},{96,64},{128,160},{160,128},{192,224},{224,1... | collective-permute-start | bytes 98312 | tf_op jit(solution)/shard_map/ppermute | solution.py:408
  4.8 3.4 %collective-permute-start = (bf16[8,16,128]{2,1,0:T(8,128)(2,1)S(1)}, bf16[8,16,128]{2,1,0:T(8,128)(2,1)S(1)}, u32[]{:S(2)}, u32[]{:S(2)}) collective-permute-start(bf16[8,16,128]{2,1,0:T(8,128)(2,1)S(1)} %get-tuple-element.22), channel_id=1, source_target_pairs={{32,64},{64,32},{96,128},{128,96},{160,192},{192,160},{224,256},{2... | collective-permute-start | bytes 98312 | tf_op jit(solution)/shard_map/ppermute | solution.py:408
  8.2 0.0 copy-done
  8.2 0.0 copy-done.2
  8.2 0.0 copy-done.1
  8.2 0.0 copy-start.3
  8.3 1.5 %shard_map.105 = (f32[16,16,256]{2,1,0:T(8,128)S(1)}, f32[16,3,16,256]{3,2,1,0:T(8,128)S(1)}, f32[12,16,256]{2,1,0:T(8,128)S(1)}) custom-call(s32[1,4096]{1,0:T(1,128)S(1)} %bitcast.8, s32[1,512]{1,0:T(1,128)S(1)} %bitcast.10, f32[3,512]{1,0:T(4,128)S(1)} %bitcast.9), custom_call_target="tpu_custom_call" | custom-call | flops 2000000000 | bytes 1245184 | tf_op jit(solution)/shard_map/pallas_call | solution.py:114
  9.8 0.0 copy-start.4
  9.8 0.0 collective-permute-done.1.from_near
  9.8 1.8 %collective-permute-done.from_far = bf16[8,16,128]{2,1,0:T(8,128)(2,1)S(1)} collective-permute-done((bf16[8,16,128]{2,1,0:T(8,128)(2,1)S(1)}, bf16[8,16,128]{2,1,0:T(8,128)(2,1)S(1)}, u32[]{:S(2)}, u32[]{:S(2)}) %collective-permute-start) | collective-permute-done | bytes 32800 | tf_op jit(solution)/shard_map/ppermute | solution.py:408
  11.5 0.0 copy-start.5
  11.6 7.8 %collective-permute-start.2 = (bf16[26,16,128]{2,1,0:T(8,128)(2,1)S(1)}, bf16[26,16,128]{2,1,0:T(8,128)(2,1)S(1)}, u32[]{:S(2)}, u32[]{:S(2)}) collective-permute-start(bf16[26,16,128]{2,1,0:T(8,128)(2,1)S(1)} %get-tuple-element.29), channel_id=1, source_target_pairs={{1,2},{2,1},{3,4},{4,3},{5,6},{6,5},{7,8},{8,7},{9,10},{10,9},{11,... | collective-permute-start | bytes 319496 | tf_op jit(solution)/shard_map/ppermute | solution.py:408
  19.4 5.4 %collective-permute-start.3 = (bf16[26,16,128]{2,1,0:T(8,128)(2,1)S(1)}, bf16[26,16,128]{2,1,0:T(8,128)(2,1)S(1)}, u32[]{:S(2)}, u32[]{:S(2)}) collective-permute-start(bf16[26,16,128]{2,1,0:T(8,128)(2,1)S(1)} %get-tuple-element.30), channel_id=1, source_target_pairs={{0,1},{1,0},{2,3},{3,2},{4,5},{5,4},{6,7},{7,6},{8,9},{9,8},{10,11... | collective-permute-start | bytes 319496 | tf_op jit(solution)/shard_map/ppermute | solution.py:408
  24.8 0.0 collective-permute-done.2.refs_4_
  24.8 0.9 %collective-permute-done.3.refs_5_ = bf16[26,16,128]{2,1,0:T(8,128)(2,1)S(1)} collective-permute-done((bf16[26,16,128]{2,1,0:T(8,128)(2,1)S(1)}, bf16[26,16,128]{2,1,0:T(8,128)(2,1)S(1)}, u32[]{:S(2)}, u32[]{:S(2)}) %collective-permute-start.3) | collective-permute-done | bytes 106528 | tf_op jit(solution)/shard_map/ppermute | solution.py:408
  25.8 0.0 copy-done.3
  25.8 0.0 copy-done.4
  25.8 0.0 copy-done.5
  25.8 7.4 %shard_map.107 = (bf16[384,128]{1,0:T(8,128)(2,1)}, f32[128,128]{1,0:T(8,128)}) custom-call(bf16[8,5,16,128]{3,2,1,0:T(8,128)(2,1)S(1)} %get-tuple-element.19.um.refs_0_, f32[8,16,128]{2,1,0:T(8,128)S(1)} %get-tuple-element.20.refs_1_, f32[8,16,128]{2,1,0:T(8,128)S(1)} %get-tuple-element.21.refs_2_, bf16[8,16,128]{2,1,0:T(8,128)(2,1)S(1)} %get-tuple-element.28.refs_3_, ...), custom_call_target="tpu_custom_call" | custom-call | flops 10000000000 | bytes 163840 | tf_op jit(solution)/shard_map/pallas_call | solution.py:114
  (1 shorter events, 0.0 us)
Async XLA Ops:
  0.6 7.6 %copy-start = (s32[4096]{0:T(1024)S(1)}, s32[4096]{0:T(1024)}, u32[]{:S(2)}) copy-start(s32[4096]{0:T(1024)} %param.12) | copy-start | bytes 49156
  0.6 7.6 %copy-start.2 = (s32[512]{0:T(512)S(1)}, s32[512]{0:T(512)}, u32[]{:S(2)}) copy-start(s32[512]{0:T(512)} %param.13) | copy-start | bytes 6148
  1.8 6.5 %copy-start.1 = (f32[512,3]{0,1:T(4,128)S(1)}, f32[512,3]{0,1:T(4,128)}, u32[]{:S(2)}) copy-start(f32[512,3]{0,1:T(4,128)} %param.14) | copy-start | bytes 18436
  1.8 8.0 %collective-permute-start.1 = (bf16[8,16,128]{2,1,0:T(8,128)(2,1)S(1)}, bf16[8,16,128]{2,1,0:T(8,128)(2,1)S(1)}, u32[]{:S(2)}, u32[]{:S(2)}) collective-permute-start(bf16[8,16,128]{2,1,0:T(8,128)(2,1)S(1)} %get-tuple-element.23), channel_id=1, source_target_pairs={{0,32},{32,0},{64,96},{96,64},{128,160},{160,128},{192,224},{224,1... | collective-permute-start | bytes 98312 | tf_op jit(solution)/shard_map/ppermute | solution.py:408
  4.8 6.8 %collective-permute-start = (bf16[8,16,128]{2,1,0:T(8,128)(2,1)S(1)}, bf16[8,16,128]{2,1,0:T(8,128)(2,1)S(1)}, u32[]{:S(2)}, u32[]{:S(2)}) collective-permute-start(bf16[8,16,128]{2,1,0:T(8,128)(2,1)S(1)} %get-tuple-element.22), channel_id=1, source_target_pairs={{32,64},{64,32},{96,128},{128,96},{160,192},{192,160},{224,256},{2... | collective-permute-start | bytes 98312 | tf_op jit(solution)/shard_map/ppermute | solution.py:408
  8.2 17.5 %copy-start.3 = (bf16[1536,128]{1,0:T(8,128)(2,1)S(1)}, bf16[1536,128]{1,0:T(8,128)(2,1)}, u32[]{:S(2)}) copy-start(bf16[1536,128]{1,0:T(8,128)(2,1)} %constant.8.clone.refs_11_) | copy-start | bytes 1179652
  9.8 16.0 %copy-start.4 = (bf16[384,192]{1,0:T(8,128)(2,1)S(1)}, bf16[384,192]{1,0:T(8,128)(2,1)}, u32[]{:S(2)}) copy-start(bf16[384,192]{1,0:T(8,128)(2,1)} %constant.6.clone.refs_9_) | copy-start | bytes 442372
  11.5 14.2 %copy-start.5 = (bf16[96,48]{1,0:T(8,128)(2,1)S(1)}, bf16[96,48]{1,0:T(8,128)(2,1)}, u32[]{:S(2)}) copy-start(bf16[96,48]{1,0:T(8,128)(2,1)} %constant.7.clone.refs_10_) | copy-start | bytes 27652
  11.6 13.2 %collective-permute-start.2 = (bf16[26,16,128]{2,1,0:T(8,128)(2,1)S(1)}, bf16[26,16,128]{2,1,0:T(8,128)(2,1)S(1)}, u32[]{:S(2)}, u32[]{:S(2)}) collective-permute-start(bf16[26,16,128]{2,1,0:T(8,128)(2,1)S(1)} %get-tuple-element.29), channel_id=1, source_target_pairs={{1,2},{2,1},{3,4},{4,3},{5,6},{6,5},{7,8},{8,7},{9,10},{10,9},{11,... | collective-permute-start | bytes 319496 | tf_op jit(solution)/shard_map/ppermute | solution.py:408
  19.4 6.4 %collective-permute-start.3 = (bf16[26,16,128]{2,1,0:T(8,128)(2,1)S(1)}, bf16[26,16,128]{2,1,0:T(8,128)(2,1)S(1)}, u32[]{:S(2)}, u32[]{:S(2)}) collective-permute-start(bf16[26,16,128]{2,1,0:T(8,128)(2,1)S(1)} %get-tuple-element.30), channel_id=1, source_target_pairs={{0,1},{1,0},{2,3},{3,2},{4,5},{5,4},{6,7},{7,6},{8,9},{9,8},{10,11... | collective-permute-start | bytes 319496 | tf_op jit(solution)/shard_map/ppermute | solution.py:408

commit v3 on v2

v3 whole, which is shorter than its diff:
```python
import math

import jax
import jax.numpy as jnp
import numpy as np
from jax import lax
from jax.experimental import pallas as pl
from jax.experimental.pallas import tpu as pltpu
from jax.sharding import PartitionSpec as P

void_modulus = 0.001
spectral_mid = 1.375
spectral_half = 1.125
sigma = spectral_mid / spectral_half
first = 1.0 / sigma
second = 1.0 / (2.0 * sigma - first)

F32, BF16, I32 = jnp.float32, jnp.bfloat16, jnp.int32
DEPTH, ROWS, COLS = 16, 8, 128
LOW, HIGH = 4, 5
WIDE, SLOT, SEAM = 256, 117, 120
OWN = COLS - SLOT
UNROLL = (8, 7, 6)
KLASS = (0, 1, 2, 4, 5, 8)


def stiffness_table():
    poisson = 0.3
    lame = poisson / ((1.0 + poisson) * (1.0 - 2.0 * poisson))
    shear = 0.5 / (1.0 + poisson)
    elastic = np.zeros((6, 6))
    elastic[:3, :3] = lame
    for index in range(3):
        elastic[index, index] += 2.0 * shear
        elastic[index + 3, index + 3] = shear
    points = [0.5 - 0.5 / math.sqrt(3.0), 0.5 + 0.5 / math.sqrt(3.0)]
    table = np.zeros((24, 24))
    for point_z in points:
        for point_y in points:
            for point_x in points:
                strain = np.zeros((6, 24))
                for corner in range(8):
                    bit_z, bit_y, bit_x = (corner // 4, corner // 2 % 2, corner % 2)
                    shape_x = point_x if bit_x else 1.0 - point_x
                    shape_y = point_y if bit_y else 1.0 - point_y
                    shape_z = point_z if bit_z else 1.0 - point_z
                    slope_x = 1.0 if bit_x else -1.0
                    slope_y = 1.0 if bit_y else -1.0
                    slope_z = 1.0 if bit_z else -1.0
                    grad_x = slope_x * shape_y * shape_z
                    grad_y = shape_x * slope_y * shape_z
                    grad_z = shape_x * shape_y * slope_z
                    strain[0, corner] = grad_x
                    strain[1, 8 + corner] = grad_y
                    strain[2, 16 + corner] = grad_z
                    strain[3, corner] = grad_y
                    strain[3, 8 + corner] = grad_x
                    strain[4, 8 + corner] = grad_z
                    strain[4, 16 + corner] = grad_y
                    strain[5, corner] = grad_z
                    strain[5, 16 + corner] = grad_x
                table += strain.T @ elastic @ strain / 8.0
    return np.asarray(table.astype(np.float32).astype(jnp.bfloat16).astype(np.float64))


def element_matrix(table):
    matrix = np.zeros((2, 2, 2, 3, DEPTH, 2, 2, 3, DEPTH))
    for corner in range(8):
        bz, by, bx = corner // 4, corner // 2 % 2, corner % 2
        for other in range(8):
            oz, oy, ox = other // 4, other // 2 % 2, other % 2
            for c in range(3):
                for k in range(3):
                    for z in range(DEPTH - 1):
                        matrix[bz, by, bx, c, z + bz, oy, ox, k, z + oz] = table[
                            c * 8 + corner, k * 8 + other
                        ]
    return matrix.reshape(384, 192)


def depth_bands():
    bands = np.zeros((6, DEPTH, 3, DEPTH))
    for z in range(DEPTH):
        for dz in range(-2, 3):
            if 0 <= z + dz < DEPTH:
                for dy in range(3):
                    bands[KLASS.index(dz * dz + dy * dy), z, dy, z + dz] = 1.0
    return bands.reshape(96, 48)


def cone(square, dx):
    return max(0.0, 3.0 - math.sqrt(square + dx * dx))


def along_bands():
    bands = np.zeros((6, WIDE, COLS))
    for k, square in enumerate(KLASS):
        for x in range(COLS):
            for dx in range(-2, 3):
                at = x + dx
                lane = at + LOW if at <= SEAM else COLS + at - SLOT
                bands[k, lane, x] = cone(square, dx)
    return bands.reshape(6 * WIDE, COLS)


def iota(shape, dim):
    return lax.broadcasted_iota(I32, shape, dim)


def starts():
    return lax.axis_index("gy") * ROWS, lax.axis_index("gx") * COLS


def call(body, outs, ins, scratch=(), flops=0, limit=None, space=pltpu.VMEM):
    whole = pl.BlockSpec(memory_space=pltpu.VMEM)
    moved = sum(math.prod(o.shape) * o.dtype.itemsize for o in outs)
    return pl.pallas_call(
        body,
        out_shape=outs,
        in_specs=[pl.BlockSpec(memory_space=space)] * len(ins),
        out_specs=[whole] * len(outs),
        scratch_shapes=list(scratch),
        compiler_params=pltpu.CompilerParams(vmem_limit_bytes=limit or (32 << 20)),
        cost_estimate=pl.CostEstimate(flops=flops, bytes_accessed=moved, transcendentals=0),
    )(*ins)


def shape_of(shape, dtype):
    return jax.ShapeDtypeStruct(shape, dtype)


def slot_of(y):
    return 16 * ((y + LOW) % 8)


def pack_body(
    grid_y, grid_x, u_in, den_in, sol_in,
    um, st_own, co_own, keep, own, far, near, u_ref, den_ref, sol_ref, uf, sem,
):
    copies = [
        pltpu.make_async_copy(source, target, sem.at[i])
        for i, (source, target) in enumerate(
            ((u_in, u_ref), (den_in, den_ref), (sol_in, sol_ref))
        )
    ]
    for copy in copies:
        copy.start()
    y0, x0 = starts()
    odd = lax.axis_index("gx") % 2 == 1
    for copy in copies:
        copy.wait()
    uf[...] = u_ref[...].astype(F32)
    lane = iota((DEPTH, COLS), 1)
    inside_zx = (iota((DEPTH, COLS), 0) < DEPTH - 1) & (lane + x0 < grid_x - 1)
    blank = jnp.zeros((DEPTH, COLS), F32)
    middle, above, below = [blank] * 5, [blank] * 5, [blank] * 5
    for y in range(ROWS):
        planes = [uf[pl.ds(c * 128 + y, DEPTH, stride=ROWS), :] for c in range(3)]
        density = den_ref[pl.ds(y, DEPTH, stride=ROWS), :]
        solid = sol_ref[pl.ds(y, DEPTH, stride=ROWS), :]
        exists = inside_zx & (y0 + y < grid_y - 1)
        physical = jnp.where(solid == 1, 1.0, density)
        square = physical * physical
        stiff = jnp.where(exists, void_modulus + (1.0 - void_modulus) * (square * physical), 0.0)
        designed = (1 - solid).astype(F32)
        factor = jnp.where(exists, (-3.0 * (1.0 - void_modulus)) * square * designed, 0.0)
        keep[y] = jnp.where(exists, designed, 0.0)
        planes += [stiff, factor]
        at = slot_of(y)
        for p, plane in enumerate(planes):
            tile = pltpu.roll(plane, LOW, 1)
            um[y, p] = tile.astype(BF16)
            if p == 3:
                st_own[y] = tile
            if p == 4:
                co_own[y] = tile
            moved = pltpu.roll(plane, at + OWN, 1)
            middle[p] = jnp.where((lane >= at) & (lane < at + OWN), moved, middle[p])
            above[p] = jnp.where((lane >= at + OWN) & (lane < at + 16), moved, above[p])
            moved = pltpu.roll(plane, (at + LOW) % COLS, 1)
            below[p] = jnp.where((lane >= at) & (lane < at + LOW), moved, below[p])
    for p in range(5):
        own[p] = middle[p].astype(BF16)
        far[p] = jnp.where(odd, below[p], above[p]).astype(BF16)
        near[p] = jnp.where(odd, above[p], below[p]).astype(BF16)


def merge_body(um, st_own, co_own, own, from_far, from_near, far, near, tiles, st, co, slots):
    odd_x = lax.axis_index("gx") % 2 == 1
    edge = iota((DEPTH, COLS), 1) < LOW
    for p in range(5):
        one, other = from_far[p].astype(F32), from_near[p].astype(F32)
        right, left = jnp.where(odd_x, one, other), jnp.where(odd_x, other, one)
        slots[p] = (own[p].astype(F32) + right).astype(BF16)
        for y in range(ROWS):
            rim = pltpu.roll(left, (COLS - slot_of(y)) % COLS, 1)
            tiles[y, p] = jnp.where(edge, rim, um[y, p].astype(F32)).astype(BF16)
            if p == 3:
                st[y] = jnp.where(edge, rim, st_own[y])
            if p == 4:
                co[y] = jnp.where(edge, rim, co_own[y])

    def fill(up, down):
        for y in range(HIGH):
            up[y * 3 : y * 3 + 3] = tiles[y, 0:3]
        up[15:19] = tiles[0:4, 3]
        up[19:21] = tiles[0:2, 4]
        up[21:26] = slots[...]
        for y in range(LOW):
            down[y * 3 : y * 3 + 3] = tiles[y + 4, 0:3]
        down[12:16] = tiles[4:8, 3]
        down[16:18] = tiles[6:8, 4]
        down[18:21] = jnp.zeros((3, DEPTH, COLS), BF16)
        down[21:26] = slots[...]

    odd = lax.axis_index("gy") % 2 == 1
    pl.when(odd)(lambda: fill(near, far))
    pl.when(jnp.logical_not(odd))(lambda: fill(far, near))


def one_hot(key, rows):
    return (iota((rows, key.shape[1]), 0) == key).astype(F32).astype(BF16)


def mask_body(
    grid_y, grid_x, fixed, nodes, forces, free, free_b, loads, loads_b, inverse, inverse_b, spread
):
    y0, x0 = starts()
    lane = iota((DEPTH, COLS), 1)

    def keys(flat):
        x = (flat & (grid_x - 1)) - x0
        y = ((flat // grid_x) & (grid_y - 1)) - y0 + LOW
        z = flat // (grid_x * grid_y)
        slot = jnp.where((x >= SLOT) & (x < SLOT + 16), x - SLOT, -1)
        places = jnp.concatenate([one_hot(x + LOW, COLS), one_hot(slot, COLS)], axis=0)
        return places, y * DEPTH + z

    def dots(a, b):
        return lax.dot_general(a, b, (((1,), (1,)), ((), ())), preferred_element_type=F32)

    def split(total):
        rows = total.reshape(16, DEPTH, WIDE)
        halves = [jnp.zeros((DEPTH, COLS), F32)] * 2
        for row in range(16):
            at = 16 * (row % 8)
            moved = pltpu.roll(rows[row, :, COLS:], at, 1)
            halves[row // 8] = jnp.where((lane >= at) & (lane < at + 16), moved, halves[row // 8])
        return rows[:, :, :COLS], jnp.concatenate(halves, axis=1)

    count = fixed.shape[1]
    part = 512
    spread[...] = jnp.zeros_like(spread)
    for at in range(0, count, part):
        kx, ky = keys(fixed[:, at : at + part])
        spread[...] += dots(one_hot(ky, 256), kx)
    free[...], free_b[...] = split(jnp.where(spread[...] > 0.0, 0.0, 1.0))

    at_x, ky = keys(nodes[...])
    here = iota((256, ky.shape[1]), 0) == ky
    for c in range(3):
        force = forces[c : c + 1, :]
        total = jnp.zeros((256, WIDE), F32)
        for _ in range(3):
            head = force.astype(BF16).astype(F32)
            total = total + dots(jnp.where(here, head, 0.0).astype(BF16), at_x)
            force = force - head
        loads[:, c], loads_b[c] = split(total)

    def within(pos, size):
        return jnp.where((pos >= 0) & (pos < size - 1), 1.0, 0.0)

    def along(xpos):
        ex = [within(xpos + d, grid_x) for d in range(-2, 3)]
        reach = {
            k: sum(cone(k, d) * ex[d + 2] for d in range(-2, 3) if cone(k, d) > 0.0)
            for k in KLASS
        }
        return ex[2], reach

    def around(pos, size):
        e = [within(pos + d, size) for d in range(-2, 3)]
        return e[2], e[1] + e[3], e[0] + e[4]

    def reciprocal(z_terms, y_terms, x_here, reach):
        total = 0.0
        for a in range(3):
            total = total + z_terms[a] * sum(y_terms[b] * reach[a * a + b * b] for b in range(3))
        alive = z_terms[0] * x_here * y_terms[0] > 0.0
        return jnp.where(alive, 1.0 / jnp.where(alive, total, 1.0), 0.0)

    x_here, reach = along(x0 + lane - LOW)
    z_terms = around(iota((DEPTH, COLS), 0), DEPTH)
    for row in range(12):
        inverse[row] = reciprocal(z_terms, around(y0 + row - 2, grid_y), x_here, reach)
    wide = iota((DEPTH, WIDE), 1)
    x_here, reach = along(x0 + SLOT + (wide & 15))
    z_terms = around(iota((DEPTH, WIDE), 0), DEPTH)
    inverse_b[...] = reciprocal(z_terms, around(y0 + (wide >> 4) - LOW, grid_y), x_here, reach)


def main_body(
    pivot, tiles, st_own, co_own, slots, keep, from_far, from_near,
    free, free_b, loads, loads_b, inverse, inverse_b, matrix, bands_z, bands_x,
    smoothed, filtered, uu, ss, vv, ub, sb, vb, st, co, res, inv, ratio, layers, out_f,
):
    odd = lax.axis_index("gy") % 2 == 1
    lane = iota((DEPTH, COLS), 1)

    def above(i):
        return jnp.where(odd, from_far[i].astype(F32), from_near[i].astype(F32))

    def below(i):
        return jnp.where(odd, from_near[i].astype(F32), from_far[i].astype(F32))

    def put(ref, row, fields):
        ref[pl.ds(row * 96, 48), :] = fields.astype(BF16)
        ref[pl.ds(row * 96 + 48, 48), :] = pltpu.roll(fields, COLS - 1, 1).astype(BF16)

    for row in range(17):
        n = row - LOW
        if n < 0:
            fields = [below(row * 3 + c) for c in range(3)]
            st[row] = below(12 + row)
            if n >= -2:
                co[row - 2] = below(14 + row)
        elif n < ROWS:
            fields = [tiles[n, c].astype(F32) for c in range(3)]
            st[row] = st_own[n]
            co[row - 2] = co_own[n]
        else:
            m = n - ROWS
            fields = [above(m * 3 + c) for c in range(3)]
            if m < 4:
                st[row] = above(15 + m)
            if m < 2:
                co[row - 2] = above(19 + m)
        put(uu, row, jnp.concatenate(fields, axis=0))

    def put_slots(ref, fields, beyond):
        after = pltpu.roll(fields, WIDE - 16, 1)
        if beyond is not None:
            last = iota(after.shape, 1) >= WIDE - 16
            after = jnp.where(last, beyond, after)
        for i, value in enumerate((fields, after)):
            ref[i * 96 : i * 96 + 48, :] = value.astype(BF16)
            ref[i * 96 + 48 : i * 96 + 96, :] = pltpu.roll(value, WIDE - 1, 1).astype(BF16)

    def side_by_side(p):
        up, mid, down = above(21 + p), slots[p].astype(F32), below(21 + p)
        joined = [jnp.where(lane < 64, down, mid), jnp.where(lane < 64, mid, up)]
        return jnp.concatenate(joined, axis=1), up

    pairs = [side_by_side(p) for p in range(5)]
    far_row = jnp.concatenate([up for _, up in pairs[:3]], axis=0)
    far_row = pltpu.roll(far_row, COLS - 16, 1)
    put_slots(
        ub,
        jnp.concatenate([f for f, _ in pairs[:3]], axis=0),
        jnp.concatenate([far_row, far_row], axis=1),
    )
    st_b, co_b = pairs[3][0], pairs[4][0]

    def product(x, stiff):
        f = jnp.dot(matrix[...], x, preferred_element_type=F32).reshape(2, 12, DEPTH, WIDE)
        g = f[0] * stiff[None] + f[1] * pltpu.roll(stiff, 1, 0)[None]
        return g.reshape(2, 2, 3 * DEPTH, WIDE)

    def two(ref, row):
        return jnp.concatenate(
            [ref[pl.ds(row * 96, 192), :], ref[pl.ds(row * 96 + 96, 192), :]], axis=1
        )

    def forces(ref, row, carry):
        g = product(two(ref, row), jnp.concatenate([st[row], st[row + 1]], axis=1))
        one = g[0, :, :, :COLS] + carry
        other = g[0, :, :, COLS:] + g[1, :, :, :COLS]
        return [h[0] + pltpu.roll(h[1], 1, 1) for h in (one, other)], g[1, :, :, COLS:]

    def forces_slots(x):
        g = product(x, st_b)
        h = g[0] + pltpu.roll(g[1].reshape(96, WIDE), 16, 1).reshape(2, 48, WIDE)
        return h[0] + pltpu.roll(h[1], 1, 1)

    def invert(both):
        diagonal = pivot * (both + pltpu.roll(both, 1, 1))
        some = diagonal > 0.0
        return jnp.where(some, 1.0 / jnp.where(some, diagonal, 1.0), 0.0)

    def step_of(residual, inverse_diagonal):
        step = (residual * (inverse_diagonal * (1.0 / spectral_mid))[None]).astype(BF16)
        return step.astype(F32).reshape(48, -1)

    def renew(old, step0, residual0, applied, mask, inverse_diagonal):
        width = mask.shape[-1]
        residual = residual0 - applied.reshape(3, DEPTH, width) * mask[None]
        step0 = step0.astype(F32).reshape(3, DEPTH, width)
        step1 = (second * first) * step0 + residual * (
            (2.0 * second / spectral_half) * inverse_diagonal
        )[None]
        new = old.astype(F32).reshape(3, DEPTH, width) + step0 + step1
        return new.astype(BF16).astype(F32).reshape(48, width)

    def first_pair(row, carry):
        before, weight = carry
        applied, after = forces(uu, row, before)
        for i in range(2):
            here = st[row + i] + pltpu.roll(st[row + i], 1, 0)
            inverse_diagonal = invert(here + weight)
            weight = here
            inv[row + i] = inverse_diagonal
            residual = loads[row + i] - applied[i].reshape(3, DEPTH, COLS)
            residual = residual * free[row + i][None]
            res[row + i] = residual
            put(ss, row + i, step_of(residual, inverse_diagonal))
        return after, weight

    zero = jnp.zeros((2, 48, COLS), F32)
    lax.fori_loop(
        0,
        8,
        lambda i, c: first_pair(2 * i, c),
        (zero, jnp.zeros((DEPTH, COLS), F32)),
        unroll=UNROLL[0],
    )
    here_b = st_b + pltpu.roll(st_b, 1, 0)
    inv_b = invert(here_b + pltpu.roll(here_b, 16, 1))
    res_b = (loads_b[...] - forces_slots(ub[...]).reshape(3, DEPTH, WIDE)) * free_b[...][None]
    put_slots(sb, step_of(res_b, inv_b), None)

    def second_pair(row, carry):
        applied, after = forces(ss, row, carry)
        for i in range(2):
            at = pl.ds((row + i) * 96, 48)
            new = renew(uu[at, :], ss[at, :], res[row + i], applied[i], free[row + i], inv[row + i])
            put(vv, row + i, new)
        return after

    lax.fori_loop(0, 7, lambda i, c: second_pair(2 * i + 1, c), zero, unroll=UNROLL[1])
    new_b = renew(ub[0:48, :], sb[0:48, :], res_b, forces_slots(sb[...]), free_b[...], inv_b)
    put_slots(vb, new_b, None)

    for y in range(ROWS):
        row, half = y + LOW, (y + LOW) // 8
        part = new_b[:, half * COLS : (half + 1) * COLS]
        part = pltpu.roll(part, (SLOT - 16 * (row % 8)) % COLS, 1)
        own = pltpu.roll(vv[row * 96 : row * 96 + 48, :].astype(F32), COLS - LOW, 1)
        own = jnp.where(iota((48, COLS), 1) <= SEAM, own, part)
        for c in range(3):
            out_f[pl.ds(c * 128 + y, DEPTH, stride=ROWS), :] = own[c * 16 : c * 16 + 16]
    smoothed[...] = out_f[...].astype(BF16)

    def energy(x):
        f = jnp.dot(matrix[...], x, preferred_element_type=F32).reshape(2, 12, DEPTH, WIDE)
        u = x.astype(F32).reshape(12, DEPTH, WIDE)
        over = jnp.sum(f[1] * u, axis=0)
        return jnp.sum(f[0] * u, axis=0) + pltpu.roll(over, DEPTH - 1, 0)

    def energy_pair(row, carry):
        value = energy(two(vv, row))
        for i in range(2):
            at = row + i - 2
            ratio[at, :, 0:COLS] = value[:, i * COLS : (i + 1) * COLS] * co[at] * inverse[at]
        return carry

    lax.fori_loop(0, 6, lambda i, c: energy_pair(2 * i + 2, c), 0, unroll=UNROLL[2])
    ratio_b = energy(vb[...]) * co_b * inverse_b[...]
    for at in range(12):
        row = at + 2
        part = ratio_b[:, (row // 8) * COLS : (row // 8 + 1) * COLS]
        ratio[at, :, COLS:WIDE] = pltpu.roll(part, (COLS - 16 * (row % 8)) % COLS, 1)

    for y in range(ROWS):
        a = jnp.concatenate(
            [ratio[y + 2], ratio[y + 1] + ratio[y + 3], ratio[y] + ratio[y + 4]], axis=0
        )
        s = jnp.dot(bands_z[...], a.astype(BF16), preferred_element_type=F32).astype(BF16)
        for k in range(6):
            layers[y * DEPTH : (y + 1) * DEPTH, k * WIDE : (k + 1) * WIDE] = s[
                k * DEPTH : (k + 1) * DEPTH
            ]
    total = jnp.dot(layers[...], bands_x[...], preferred_element_type=F32)
    for y in range(ROWS):
        filtered[pl.ds(y, DEPTH, stride=ROWS), :] = total[y * DEPTH : (y + 1) * DEPTH] * keep[y]


def main_scratch():
    return [
        pltpu.VMEM((17 * 96, COLS), BF16),
        pltpu.VMEM((16 * 96, COLS), BF16),
        pltpu.VMEM((15 * 96, COLS), BF16),
        pltpu.VMEM((192, WIDE), BF16),
        pltpu.VMEM((192, WIDE), BF16),
        pltpu.VMEM((192, WIDE), BF16),
        pltpu.VMEM((16, DEPTH, COLS), F32),
        pltpu.VMEM((12, DEPTH, COLS), F32),
        pltpu.VMEM((16, 3, DEPTH, COLS), F32),
        pltpu.VMEM((16, DEPTH, COLS), F32),
        pltpu.VMEM((12, DEPTH, WIDE), F32),
        pltpu.VMEM((128, 6 * WIDE), BF16),
        pltpu.VMEM((384, 128), F32),
    ]


def swapped(shard, axis, odd):
    size = lax.axis_size(axis)
    partner = [((i - odd) ^ 1) + odd for i in range(size)]
    return lax.ppermute(shard, axis, [(i, j) for i, j in enumerate(partner) if 0 <= j < size])


def shards(displacement, density, solid, fixed_nodes, load_nodes, load_forces):
    grid_y = ROWS * lax.axis_size("gy")
    grid_x = COLS * lax.axis_size("gx")
    table = stiffness_table()
    pivot = float(table[0, 0])
    tile = (DEPTH, COLS)

    given = (
        displacement.reshape(384, 128),
        density.reshape(128, 128),
        solid.reshape(128, 128),
    )
    um, st_own, co_own, keep, own, far, near = call(
        lambda *refs: pack_body(grid_y, grid_x, *refs),
        [
            shape_of((ROWS, 5) + tile, BF16),
            shape_of((ROWS,) + tile, F32),
            shape_of((ROWS,) + tile, F32),
            shape_of((ROWS,) + tile, F32),
            shape_of((5,) + tile, BF16),
            shape_of((5,) + tile, BF16),
            shape_of((5,) + tile, BF16),
        ],
        [pltpu.with_memory_space_constraint(array, pltpu.HBM) for array in given],
        [
            pltpu.VMEM((384, 128), BF16),
            pltpu.VMEM((128, 128), F32),
            pltpu.VMEM((128, 128), I32),
            pltpu.VMEM((384, 128), F32),
            pltpu.SemaphoreType.DMA((3,)),
        ],
        space=pltpu.HBM,
    )
    nodes, _ = lax.optimization_barrier((fixed_nodes, far))
    from_far = swapped(far, "gx", 1)
    from_near = swapped(near, "gx", 0)
    masks = call(
        lambda *refs: mask_body(grid_y, grid_x, *refs),
        [
            shape_of((16,) + tile, F32),
            shape_of((DEPTH, WIDE), F32),
            shape_of((16, 3) + tile, F32),
            shape_of((3, DEPTH, WIDE), F32),
            shape_of((12,) + tile, F32),
            shape_of((DEPTH, WIDE), F32),
        ],
        [nodes.reshape(1, -1), load_nodes.reshape(1, -1), load_forces.T],
        [pltpu.VMEM((256, WIDE), F32)],
        flops=2000000000,
    )
    from_far, from_near, masks = lax.optimization_barrier((from_far, from_near, masks))
    far, near, tiles, st, co, slots = call(
        merge_body,
        [
            shape_of((26,) + tile, BF16),
            shape_of((26,) + tile, BF16),
            shape_of((ROWS, 5) + tile, BF16),
            shape_of((ROWS,) + tile, F32),
            shape_of((ROWS,) + tile, F32),
            shape_of((5,) + tile, BF16),
        ],
        [um, st_own, co_own, own, from_far, from_near],
    )
    from_far = swapped(far, "gy", 1)
    from_near = swapped(near, "gy", 0)
    smoothed, filtered = call(
        lambda *refs: main_body(pivot, *refs),
        [shape_of((384, 128), BF16), shape_of((128, 128), F32)],
        [
            tiles,
            st,
            co,
            slots,
            keep,
            from_far,
            from_near,
            *masks,
            jnp.asarray(element_matrix(table), BF16),
            jnp.asarray(depth_bands(), BF16),
            jnp.asarray(along_bands(), BF16),
        ],
        main_scratch(),
        flops=10000000000,
    )
    return smoothed.reshape(3, DEPTH, ROWS, COLS), filtered.reshape(DEPTH, ROWS, COLS)


def solution(mesh):
    placed = (P(None, None, "gy", "gx"), P(None, "gy", "gx"), P(None, "gy", "gx"), P(), P(), P())
    return jax.shard_map(
        shards,
        mesh=mesh,
        in_specs=placed,
        out_specs=(P(None, None, "gy", "gx"), P(None, "gy", "gx")),
        check_vma=False,
    )
```

time: 33.4 us -> 29.4 us (0.88)
  Pallas kernels: 10 us -> 6.17 us
    pallas_call x4, Pallas kernels: 10 us -> 6.17 us  [call(): pl.pallas_call(body, out_shape=outs, in_specs=[pl.BlockSpec(memory_space=...]
where the time goes in v3:
time: 29.4 us; the launch traced here: 29.1 us
  starting transfers between devices  19.6 us (67%)
  Pallas kernels  6.17 us (21%)
  waiting for transfers between devices  2.5 us (9%)
  between operations  0.77 us (3%)
    ppermute x4, starting transfers between devices, swapped(): lax.ppermute(shard, axis, [(i, j) for i, j in enumerate(partner) if 0 <=...  19.6 us
    pallas_call x4, Pallas kernels, call(): pl.pallas_call(body, out_shape=outs, in_specs=[pl.BlockSpec(memory_space=...  6.17 us
    ppermute x4, waiting for transfers between devices, swapped(): lax.ppermute(shard, axis, [(i, j) for i, j in enumerate(partner) if 0 <=...  2.5 us
  transfers between devices with their start and end apart: 4, of which 2 were waited for; matrix products, arithmetic and copies ran while one was open for 0% of the time, Pallas kernels for 5%

profile of v3, /device:TPU:63, one launch (start us, length us, event | category | flops | bytes accessed | tf_op | source)
XLA Modules:
  0.0 29.1 jit_solution(16310273314962906551)
XLA Ops:
  0.6 0.0 copy-start
  0.6 0.0 copy-start.2
  0.7 1.2 %shard_map.104 = (bf16[8,5,16,128]{3,2,1,0:T(8,128)(2,1)S(1)}, f32[8,16,128]{2,1,0:T(8,128)S(1)}, f32[8,16,128]{2,1,0:T(8,128)S(1)}, f32[8,16,128]{2,1,0:T(8,128...) custom-call(bf16[384,128]{1,0:T(8,128)(2,1)} %bitcast.11, ...), custom_call_target="tpu_custom_call" | custom-call | bytes 421888 | tf_op jit(solution)/shard_map/pallas_call | solution.py:117
  1.8 0.0 copy-start.1
  1.8 3.0 %collective-permute-start.1 = (bf16[5,16,128]{2,1,0:T(8,128)(2,1)S(1)}, bf16[5,16,128]{2,1,0:T(8,128)(2,1)S(1)}, u32[]{:S(2)}, u32[]{:S(2)}) collective-permute-start(bf16[5,16,128]{2,1,0:T(8,128)(2,1)S(1)} %get-tuple-element.37), channel_id=1, source_target_pairs={{0,32},{32,0},{64,96},{96,64},{128,160},{160,128},{192,224},{224,1... | collective-permute-start | bytes 61448 | tf_op jit(solution)/shard_map/ppermute | solution.py:508
  4.8 3.4 %collective-permute-start = (bf16[5,16,128]{2,1,0:T(8,128)(2,1)S(1)}, bf16[5,16,128]{2,1,0:T(8,128)(2,1)S(1)}, u32[]{:S(2)}, u32[]{:S(2)}) collective-permute-start(bf16[5,16,128]{2,1,0:T(8,128)(2,1)S(1)} %get-tuple-element.36), channel_id=1, source_target_pairs={{32,64},{64,32},{96,128},{128,96},{160,192},{192,160},{224,256},{2... | collective-permute-start | bytes 61448 | tf_op jit(solution)/shard_map/ppermute | solution.py:508
  8.3 0.0 copy-done
  8.3 0.0 copy-done.2
  8.3 0.0 copy-done.1
  8.3 0.0 copy-start.3
  8.3 1.6 %shard_map.105 = (f32[16,16,128]{2,1,0:T(8,128)S(1)}, f32[16,256]{1,0:T(8,128)S(1)}, f32[16,3,16,128]{3,2,1,0:T(8,128)S(1)}, f32[3,16,256]{2,1,0:T(8,128)S(1)}, ...) custom-call(s32[1,4096]{1,0:T(1,128)S(1)} %bitcast.8, s32[1,512]{1,0:T(1,128)S(1)} %bitcast.10, f32[3,512]{1,0:T(4,128)S(1)} %bitcast.9), custom_call_target="tpu_custom_call" | custom-call | flops 2000000000 | bytes 704512 | tf_op jit(solution)/shard_map/pallas_call | solution.py:117
  9.9 0.0 copy-start.4
  9.9 0.0 collective-permute-done.1.from_near
  9.9 1.6 %collective-permute-done.from_far = bf16[5,16,128]{2,1,0:T(8,128)(2,1)S(1)} collective-permute-done((bf16[5,16,128]{2,1,0:T(8,128)(2,1)S(1)}, bf16[5,16,128]{2,1,0:T(8,128)(2,1)S(1)}, u32[]{:S(2)}, u32[]{:S(2)}) %collective-permute-start) | collective-permute-done | bytes 20512 | tf_op jit(solution)/shard_map/ppermute | solution.py:508
  11.5 0.0 copy-start.5
  11.5 0.1 shard_map.106
  11.6 7.8 %collective-permute-start.2 = (bf16[26,16,128]{2,1,0:T(8,128)(2,1)S(1)}, bf16[26,16,128]{2,1,0:T(8,128)(2,1)S(1)}, u32[]{:S(2)}, u32[]{:S(2)}) collective-permute-start(bf16[26,16,128]{2,1,0:T(8,128)(2,1)S(1)} %get-tuple-element.52), channel_id=1, source_target_pairs={{1,2},{2,1},{3,4},{4,3},{5,6},{6,5},{7,8},{8,7},{9,10},{10,9},{11,... | collective-permute-start | bytes 319496 | tf_op jit(solution)/shard_map/ppermute | solution.py:508
  19.4 5.4 %collective-permute-start.3 = (bf16[26,16,128]{2,1,0:T(8,128)(2,1)S(1)}, bf16[26,16,128]{2,1,0:T(8,128)(2,1)S(1)}, u32[]{:S(2)}, u32[]{:S(2)}) collective-permute-start(bf16[26,16,128]{2,1,0:T(8,128)(2,1)S(1)} %get-tuple-element.53), channel_id=1, source_target_pairs={{0,1},{1,0},{2,3},{3,2},{4,5},{5,4},{6,7},{7,6},{8,9},{9,8},{10,11... | collective-permute-start | bytes 319496 | tf_op jit(solution)/shard_map/ppermute | solution.py:508
  24.9 0.0 collective-permute-done.2.refs_5_
  24.9 0.9 %collective-permute-done.3.refs_6_ = bf16[26,16,128]{2,1,0:T(8,128)(2,1)S(1)} collective-permute-done((bf16[26,16,128]{2,1,0:T(8,128)(2,1)S(1)}, bf16[26,16,128]{2,1,0:T(8,128)(2,1)S(1)}, u32[]{:S(2)}, u32[]{:S(2)}) %collective-permute-start.3) | collective-permute-done | bytes 106528 | tf_op jit(solution)/shard_map/ppermute | solution.py:508
  25.8 0.0 copy-done.3
  25.8 0.0 copy-done.4
  25.8 0.0 copy-done.5
  25.8 3.3 %shard_map.107 = (bf16[384,128]{1,0:T(8,128)(2,1)}, f32[128,128]{1,0:T(8,128)}) custom-call(bf16[8,5,16,128]{3,2,1,0:T(8,128)(2,1)S(1)} %get-tuple-element.47.refs_0_, f32[8,16,128]{2,1,0:T(8,128)S(1)} %get-tuple-element.48.refs_1_, f32[8,16,128]{2,1,0:T(8,128)S(1)} %get-tuple-element.49.refs_2_, bf16[5,16,128]{2,1,0:T(8,128)(2,1)S(1)} %get-tuple-element.50.refs_3_, ...), custom_call_target="tpu_custom_call" | custom-call | flops 10000000000 | bytes 163840 | tf_op jit(solution)/shard_map/pallas_call | solution.py:117
Async XLA Ops:
  0.6 7.6 %copy-start = (s32[4096]{0:T(1024)S(1)}, s32[4096]{0:T(1024)}, u32[]{:S(2)}) copy-start(s32[4096]{0:T(1024)} %param.12) | copy-start | bytes 49156
  0.6 7.6 %copy-start.2 = (s32[512]{0:T(512)S(1)}, s32[512]{0:T(512)}, u32[]{:S(2)}) copy-start(s32[512]{0:T(512)} %param.13) | copy-start | bytes 6148
  1.8 6.5 %copy-start.1 = (f32[512,3]{0,1:T(4,128)S(1)}, f32[512,3]{0,1:T(4,128)}, u32[]{:S(2)}) copy-start(f32[512,3]{0,1:T(4,128)} %param.14) | copy-start | bytes 18436
  1.8 8.0 %collective-permute-start.1 = (bf16[5,16,128]{2,1,0:T(8,128)(2,1)S(1)}, bf16[5,16,128]{2,1,0:T(8,128)(2,1)S(1)}, u32[]{:S(2)}, u32[]{:S(2)}) collective-permute-start(bf16[5,16,128]{2,1,0:T(8,128)(2,1)S(1)} %get-tuple-element.37), channel_id=1, source_target_pairs={{0,32},{32,0},{64,96},{96,64},{128,160},{160,128},{192,224},{224,1... | collective-permute-start | bytes 61448 | tf_op jit(solution)/shard_map/ppermute | solution.py:508
  4.8 6.6 %collective-permute-start = (bf16[5,16,128]{2,1,0:T(8,128)(2,1)S(1)}, bf16[5,16,128]{2,1,0:T(8,128)(2,1)S(1)}, u32[]{:S(2)}, u32[]{:S(2)}) collective-permute-start(bf16[5,16,128]{2,1,0:T(8,128)(2,1)S(1)} %get-tuple-element.36), channel_id=1, source_target_pairs={{32,64},{64,32},{96,128},{128,96},{160,192},{192,160},{224,256},{2... | collective-permute-start | bytes 61448 | tf_op jit(solution)/shard_map/ppermute | solution.py:508
  8.3 17.5 %copy-start.3 = (bf16[1536,128]{1,0:T(8,128)(2,1)S(1)}, bf16[1536,128]{1,0:T(8,128)(2,1)}, u32[]{:S(2)}) copy-start(bf16[1536,128]{1,0:T(8,128)(2,1)} %constant.8.clone.refs_15_) | copy-start | bytes 1179652
  9.9 15.9 %copy-start.4 = (bf16[384,192]{1,0:T(8,128)(2,1)S(1)}, bf16[384,192]{1,0:T(8,128)(2,1)}, u32[]{:S(2)}) copy-start(bf16[384,192]{1,0:T(8,128)(2,1)} %constant.6.clone.refs_13_) | copy-start | bytes 442372
  11.5 14.3 %copy-start.5 = (bf16[96,48]{1,0:T(8,128)(2,1)S(1)}, bf16[96,48]{1,0:T(8,128)(2,1)}, u32[]{:S(2)}) copy-start(bf16[96,48]{1,0:T(8,128)(2,1)} %constant.7.clone.refs_14_) | copy-start | bytes 27652
  11.6 13.2 %collective-permute-start.2 = (bf16[26,16,128]{2,1,0:T(8,128)(2,1)S(1)}, bf16[26,16,128]{2,1,0:T(8,128)(2,1)S(1)}, u32[]{:S(2)}, u32[]{:S(2)}) collective-permute-start(bf16[26,16,128]{2,1,0:T(8,128)(2,1)S(1)} %get-tuple-element.52), channel_id=1, source_target_pairs={{1,2},{2,1},{3,4},{4,3},{5,6},{6,5},{7,8},{8,7},{9,10},{10,9},{11,... | collective-permute-start | bytes 319496 | tf_op jit(solution)/shard_map/ppermute | solution.py:508
  19.4 6.4 %collective-permute-start.3 = (bf16[26,16,128]{2,1,0:T(8,128)(2,1)S(1)}, bf16[26,16,128]{2,1,0:T(8,128)(2,1)S(1)}, u32[]{:S(2)}, u32[]{:S(2)}) collective-permute-start(bf16[26,16,128]{2,1,0:T(8,128)(2,1)S(1)} %get-tuple-element.53), channel_id=1, source_target_pairs={{0,1},{1,0},{2,3},{3,2},{4,5},{5,4},{6,7},{7,6},{8,9},{9,8},{10,11... | collective-permute-start | bytes 319496 | tf_op jit(solution)/shard_map/ppermute | solution.py:508

commit v4 on v3

--- a/solution.py
+++ b/solution.py
@@ -20,6 +20,7 @@
 LOW, HIGH = 4, 5
 WIDE, SLOT, SEAM = 256, 117, 120
 OWN = COLS - SLOT
+PARTS = 2
 UNROLL = (8, 7, 6)
 KLASS = (0, 1, 2, 4, 5, 8)
 
@@ -133,20 +134,57 @@
     return 16 * ((y + LOW) % 8)
 
 
+def weigh(grid_y, grid_x, inverse, inverse_b):
+    y0, x0 = starts()
+    lane = iota((DEPTH, COLS), 1)
+
+    def within(pos, size):
+        return jnp.where((pos >= 0) & (pos < size - 1), 1.0, 0.0)
+
+    def along(xpos):
+        ex = [within(xpos + d, grid_x) for d in range(-2, 3)]
+        reach = {
+            k: sum(cone(k, d) * ex[d + 2] for d in range(-2, 3) if cone(k, d) > 0.0)
+            for k in KLASS
+        }
+        return ex[2], reach
+
+    def around(pos, size):
+        e = [within(pos + d, size) for d in range(-2, 3)]
+        return e[2], e[1] + e[3], e[0] + e[4]
+
+    def reciprocal(z_terms, y_terms, x_here, reach):
+        total = 0.0
+        for a in range(3):
+            total = total + z_terms[a] * sum(y_terms[b] * reach[a * a + b * b] for b in range(3))
+        alive = z_terms[0] * x_here * y_terms[0] > 0.0
+        return jnp.where(alive, 1.0 / jnp.where(alive, total, 1.0), 0.0)
+
+    x_here, reach = along(x0 + lane - LOW)
+    z_terms = around(iota((DEPTH, COLS), 0), DEPTH)
+    for row in range(12):
+        inverse[row] = reciprocal(z_terms, around(y0 + row - 2, grid_y), x_here, reach)
+    wide = iota((DEPTH, WIDE), 1)
+    x_here, reach = along(x0 + SLOT + (wide & 15))
+    z_terms = around(iota((DEPTH, WIDE), 0), DEPTH)
+    inverse_b[...] = reciprocal(z_terms, around(y0 + (wide >> 4) - LOW, grid_y), x_here, reach)
+
+
 def pack_body(
-    grid_y, grid_x, u_in, den_in, sol_in,
-    um, st_own, co_own, keep, own, far, near, u_ref, den_ref, sol_ref, uf, sem,
+    grid_y, grid_x, u_in, den_in, sol_in, nodes_in,
+    um, st_own, co_own, keep, own, far, near, inverse, inverse_b, nodes, u_ref, den_ref, sol_ref, uf, sem,
 ):
     copies = [
         pltpu.make_async_copy(source, target, sem.at[i])
         for i, (source, target) in enumerate(
-            ((u_in, u_ref), (den_in, den_ref), (sol_in, sol_ref))
+            ((u_in, u_ref), (den_in, den_ref), (sol_in, sol_ref), (nodes_in, nodes))
         )
     ]
     for copy in copies:
         copy.start()
     y0, x0 = starts()
     odd = lax.axis_index("gx") % 2 == 1
+    weigh(grid_y, grid_x, inverse, inverse_b)
     for copy in copies:
         copy.wait()
     uf[...] = u_ref[...].astype(F32)
@@ -166,19 +204,15 @@
         factor = jnp.where(exists, (-3.0 * (1.0 - void_modulus)) * square * designed, 0.0)
         keep[y] = jnp.where(exists, designed, 0.0)
         planes += [stiff, factor]
+        st_own[y], co_own[y] = stiff, factor
         at = slot_of(y)
         for p, plane in enumerate(planes):
-            tile = pltpu.roll(plane, LOW, 1)
-            um[y, p] = tile.astype(BF16)
-            if p == 3:
-                st_own[y] = tile
-            if p == 4:
-                co_own[y] = tile
+            if p < 3:
+                um[y, p] = plane.astype(BF16)
             moved = pltpu.roll(plane, at + OWN, 1)
             middle[p] = jnp.where((lane >= at) & (lane < at + OWN), moved, middle[p])
             above[p] = jnp.where((lane >= at + OWN) & (lane < at + 16), moved, above[p])
-            moved = pltpu.roll(plane, (at + LOW) % COLS, 1)
-            below[p] = jnp.where((lane >= at) & (lane < at + LOW), moved, below[p])
+            below[p] = jnp.where((lane >= at + OWN - LOW) & (lane < at + OWN), moved, below[p])
     for p in range(5):
         own[p] = middle[p].astype(BF16)
         far[p] = jnp.where(odd, below[p], above[p]).astype(BF16)
@@ -193,7 +227,7 @@
         right, left = jnp.where(odd_x, one, other), jnp.where(odd_x, other, one)
         slots[p] = (own[p].astype(F32) + right).astype(BF16)
         for y in range(ROWS):
-            rim = pltpu.roll(left, (COLS - slot_of(y)) % COLS, 1)
+            rim = pltpu.roll(left, (COLS - slot_of(y) - OWN + LOW) % COLS, 1)
             tiles[y, p] = jnp.where(edge, rim, um[y, p].astype(F32)).astype(BF16)
             if p == 3:
                 st[y] = jnp.where(edge, rim, st_own[y])
@@ -222,81 +256,58 @@
     return (iota((rows, key.shape[1]), 0) == key).astype(F32).astype(BF16)
 
 
-def mask_body(
-    grid_y, grid_x, fixed, nodes, forces, free, free_b, loads, loads_b, inverse, inverse_b, spread
-):
+def places(grid_y, grid_x, flat):
     y0, x0 = starts()
+    x = (flat & (grid_x - 1)) - x0
+    y = ((flat // grid_x) & (grid_y - 1)) - y0 + LOW
+    z = flat // (grid_x * grid_y)
+    slot = jnp.where((x >= SLOT) & (x < SLOT + 16), x - SLOT, -1)
+    along = jnp.concatenate([one_hot(x + LOW, COLS), one_hot(slot, COLS)], axis=0)
+    return along, y * DEPTH + z
+
+
+def dots(a, b):
+    return lax.dot_general(a, b, (((1,), (1,)), ((), ())), preferred_element_type=F32)
+
+
+def split(total):
     lane = iota((DEPTH, COLS), 1)
-
-    def keys(flat):
-        x = (flat & (grid_x - 1)) - x0
-        y = ((flat // grid_x) & (grid_y - 1)) - y0 + LOW
-        z = flat // (grid_x * grid_y)
-        slot = jnp.where((x >= SLOT) & (x < SLOT + 16), x - SLOT, -1)
-        places = jnp.concatenate([one_hot(x + LOW, COLS), one_hot(slot, COLS)], axis=0)
-        return places, y * DEPTH + z
-
-    def dots(a, b):
-        return lax.dot_general(a, b, (((1,), (1,)), ((), ())), preferred_element_type=F32)
-
-    def split(total):
-        rows = total.reshape(16, DEPTH, WIDE)
-        halves = [jnp.zeros((DEPTH, COLS), F32)] * 2
-        for row in range(16):
-            at = 16 * (row % 8)
-            moved = pltpu.roll(rows[row, :, COLS:], at, 1)
-            halves[row // 8] = jnp.where((lane >= at) & (lane < at + 16), moved, halves[row // 8])
-        return rows[:, :, :COLS], jnp.concatenate(halves, axis=1)
-
+    rows = total.reshape(16, DEPTH, WIDE)
+    halves = [jnp.zeros((DEPTH, COLS), F32)] * 2
+    for row in range(16):
+        at = 16 * (row % 8)
+        moved = pltpu.roll(rows[row, :, COLS:], at, 1)
+        halves[row // 8] = jnp.where((lane >= at) & (lane < at + 16), moved, halves[row // 8])
+    return rows[:, :, :COLS], jnp.concatenate(halves, axis=1)
+
+
+def load_body(grid_y, grid_x, nodes, forces, um, st, co, loads, loads_b, tiles, st_own, co_own):
+    for y in range(ROWS):
+        planes = [um[y, c].astype(F32) for c in range(3)] + [st[y], co[y]]
+        planes = [pltpu.roll(plane, LOW, 1) for plane in planes]
+        for p, plane in enumerate(planes):
+            tiles[y, p] = plane.astype(BF16)
+        st_own[y], co_own[y] = planes[3:]
+    at_x, ky = places(grid_y, grid_x, nodes[...])
+    here = iota((256, ky.shape[1]), 0) == ky
+    for c in range(3):
+        force = forces[c : c + 1, :]
+        total = jnp.zeros((256, WIDE), F32)
+        for _ in range(PARTS):
+            head = force.astype(BF16).astype(F32)
+            total = total + dots(jnp.where(here, head, 0.0).astype(BF16), at_x)
+            force = force - head
+        loads[:, c], loads_b[c] = split(total)
+
+
+def mask_body(grid_y, grid_x, fixed, free, free_b, spread):
     count = fixed.shape[1]
     part = 512
     spread[...] = jnp.zeros_like(spread)
     for at in range(0, count, part):
-        kx, ky = keys(fixed[:, at : at + part])
+        kx, ky = places(grid_y, grid_x, fixed[:, at : at + part])
         spread[...] += dots(one_hot(ky, 256), kx)
     free[...], free_b[...] = split(jnp.where(spread[...] > 0.0, 0.0, 1.0))
-
-    at_x, ky = keys(nodes[...])
-    here = iota((256, ky.shape[1]), 0) == ky
-    for c in range(3):
-        force = forces[c : c + 1, :]
-        total = jnp.zeros((256, WIDE), F32)
-        for _ in range(3):
-            head = force.astype(BF16).astype(F32)
-            total = total + dots(jnp.where(here, head, 0.0).astype(BF16), at_x)
-            force = force - head
-        loads[:, c], loads_b[c] = split(total)
-
-    def within(pos, size):
-        return jnp.where((pos >= 0) & (pos < size - 1), 1.0, 0.0)
-
-    def along(xpos):
-        ex = [within(xpos + d, grid_x) for d in range(-2, 3)]
-        reach = {
-            k: sum(cone(k, d) * ex[d + 2] for d in range(-2, 3) if cone(k, d) > 0.0)
-            for k in KLASS
-        }
-        return ex[2], reach
-
-    def around(pos, size):
-        e = [within(pos + d, size) for d in range(-2, 3)]
-        return e[2], e[1] + e[3], e[0] + e[4]
-
-    def reciprocal(z_terms, y_terms, x_here, reach):
-        total = 0.0
-        for a in range(3):
-            total = total + z_terms[a] * sum(y_terms[b] * reach[a * a + b * b] for b in range(3))
-        alive = z_terms[0] * x_here * y_terms[0] > 0.0
-        return jnp.where(alive, 1.0 / jnp.where(alive, total, 1.0), 0.0)
-
-    x_here, reach = along(x0 + lane - LOW)
-    z_terms = around(iota((DEPTH, COLS), 0), DEPTH)
-    for row in range(12):
-        inverse[row] = reciprocal(z_terms, around(y0 + row - 2, grid_y), x_here, reach)
-    wide = iota((DEPTH, WIDE), 1)
-    x_here, reach = along(x0 + SLOT + (wide & 15))
-    z_terms = around(iota((DEPTH, WIDE), 0), DEPTH)
-    inverse_b[...] = reciprocal(z_terms, around(y0 + (wide >> 4) - LOW, grid_y), x_here, reach)
 
 
 def main_body(
@@ -519,17 +530,21 @@
         displacement.reshape(384, 128),
         density.reshape(128, 128),
         solid.reshape(128, 128),
-    )
-    um, st_own, co_own, keep, own, far, near = call(
+        load_nodes.reshape(1, -1),
+    )
+    um, st, co, keep, own, far, near, inverse, inverse_b, nodes = call(
         lambda *refs: pack_body(grid_y, grid_x, *refs),
         [
-            shape_of((ROWS, 5) + tile, BF16),
+            shape_of((ROWS, 3) + tile, BF16),
             shape_of((ROWS,) + tile, F32),
             shape_of((ROWS,) + tile, F32),
             shape_of((ROWS,) + tile, F32),
             shape_of((5,) + tile, BF16),
             shape_of((5,) + tile, BF16),
             shape_of((5,) + tile, BF16),
+            shape_of((12,) + tile, F32),
+            shape_of((DEPTH, WIDE), F32),
+            shape_of((1, load_nodes.shape[0]), I32),
         ],
         [pltpu.with_memory_space_constraint(array, pltpu.HBM) for array in given],
         [
@@ -537,28 +552,26 @@
             pltpu.VMEM((128, 128), F32),
             pltpu.VMEM((128, 128), I32),
             pltpu.VMEM((384, 128), F32),
-            pltpu.SemaphoreType.DMA((3,)),
+            pltpu.SemaphoreType.DMA((4,)),
         ],
         space=pltpu.HBM,
     )
-    nodes, _ = lax.optimization_barrier((fixed_nodes, far))
+    st, _ = lax.optimization_barrier((st, near))
     from_far = swapped(far, "gx", 1)
     from_near = swapped(near, "gx", 0)
-    masks = call(
-        lambda *refs: mask_body(grid_y, grid_x, *refs),
+    *loads, um, st, co = call(
+        lambda *refs: load_body(grid_y, grid_x, *refs),
         [
-            shape_of((16,) + tile, F32),
-            shape_of((DEPTH, WIDE), F32),
             shape_of((16, 3) + tile, F32),
             shape_of((3, DEPTH, WIDE), F32),
-            shape_of((12,) + tile, F32),
-            shape_of((DEPTH, WIDE), F32),
+            shape_of((ROWS, 5) + tile, BF16),
+            shape_of((ROWS,) + tile, F32),
+            shape_of((ROWS,) + tile, F32),
         ],
-        [nodes.reshape(1, -1), load_nodes.reshape(1, -1), load_forces.T],
-        [pltpu.VMEM((256, WIDE), F32)],
-        flops=2000000000,
-    )
-    from_far, from_near, masks = lax.optimization_barrier((from_far, from_near, masks))
+        [nodes, load_forces.T, um, st, co],
+        flops=1000000000,
+    )
+    from_far, from_near, um = lax.optimization_barrier((from_far, from_near, um))
     far, near, tiles, st, co, slots = call(
         merge_body,
         [
@@ -569,10 +582,21 @@
             shape_of((ROWS,) + tile, F32),
             shape_of((5,) + tile, BF16),
         ],
-        [um, st_own, co_own, own, from_far, from_near],
-    )
+        [um, st, co, own, from_far, from_near],
+    )
+    fixed, _ = lax.optimization_barrier((fixed_nodes, near))
     from_far = swapped(far, "gy", 1)
     from_near = swapped(near, "gy", 0)
+    free, free_b = call(
+        lambda *refs: mask_body(grid_y, grid_x, *refs),
+        [
+            shape_of((16,) + tile, F32),
+            shape_of((DEPTH, WIDE), F32),
+        ],
+        [fixed.reshape(1, -1)],
+        [pltpu.VMEM((256, WIDE), F32)],
+        flops=1000000000,
+    )
     smoothed, filtered = call(
         lambda *refs: main_body(pivot, *refs),
         [shape_of((384, 128), BF16), shape_of((128, 128), F32)],
@@ -584,7 +608,11 @@
             keep,
             from_far,
             from_near,
-            *masks,
+            free,
+            free_b,
+            *loads,
+            inverse,
+            inverse_b,
             jnp.asarray(element_matrix(table), BF16),
             jnp.asarray(depth_bands(), BF16),
             jnp.asarray(along_bands(), BF16),

time: 29.4 us -> 28.9 us (0.983)
  the two profiles are of different devices: /device:TPU:63 before, /device:TPU:31 now
where the time goes in v4:
time: 28.9 us; the launch traced here: 28.6 us
  starting transfers between devices  19.6 us (68%)
  Pallas kernels  6.36 us (22%)
  waiting for transfers between devices  1.88 us (7%)
  between operations  0.78 us (3%)
    ppermute x4, starting transfers between devices, swapped(): lax.ppermute(shard, axis, [(i, j) for i, j in enumerate(partner) if 0 <=...  19.6 us
    pallas_call x5, Pallas kernels, call(): pl.pallas_call(body, out_shape=outs, in_specs=[pl.BlockSpec(memory_space=...  6.36 us
    ppermute x4, waiting for transfers between devices, swapped(): lax.ppermute(shard, axis, [(i, j) for i, j in enumerate(partner) if 0 <=...  1.88 us
  transfers between devices with their start and end apart: 4, of which 1 were waited for; matrix products, arithmetic and copies ran while one was open for 0% of the time, Pallas kernels for 6%

profile of v4, /device:TPU:31, one launch (start us, length us, event | category | flops | bytes accessed | tf_op | source)
XLA Modules:
  0.0 28.6 jit_solution(13239304019815368430)
XLA Ops:
  0.6 1.1 %shard_map.104 = (bf16[8,3,16,128]{3,2,1,0:T(8,128)(2,1)S(1)}, f32[8,16,128]{2,1,0:T(8,128)S(1)}, f32[8,16,128]{2,1,0:T(8,128)S(1)}, f32[8,16,128]{2,1,0:T(8,128...) custom-call(bf16[384,128]{1,0:T(8,128)(2,1)} %bitcast.10, ...), custom_call_target="tpu_custom_call" | custom-call | bytes 473088 | tf_op jit(solution)/shard_map/pallas_call | solution.py:118
  1.8 0.0 copy-start.1
  1.8 4.4 %collective-permute-start = (bf16[5,16,128]{2,1,0:T(8,128)(2,1)S(1)}, bf16[5,16,128]{2,1,0:T(8,128)(2,1)S(1)}, u32[]{:S(2)}, u32[]{:S(2)}) collective-permute-start(bf16[5,16,128]{2,1,0:T(8,128)(2,1)S(1)} %get-tuple-element.32), channel_id=1, source_target_pairs={{32,64},{64,32},{96,128},{128,96},{160,192},{192,160},{224,256},{2... | collective-permute-start | bytes 61448 | tf_op jit(solution)/shard_map/ppermute | solution.py:519
  6.2 1.9 %collective-permute-start.1 = (bf16[5,16,128]{2,1,0:T(8,128)(2,1)S(1)}, bf16[5,16,128]{2,1,0:T(8,128)(2,1)S(1)}, u32[]{:S(2)}, u32[]{:S(2)}) collective-permute-start(bf16[5,16,128]{2,1,0:T(8,128)(2,1)S(1)} %get-tuple-element.33), channel_id=1, source_target_pairs={{0,32},{32,0},{64,96},{96,64},{128,160},{160,128},{192,224},{224,1... | collective-permute-start | bytes 61448 | tf_op jit(solution)/shard_map/ppermute | solution.py:519
  8.1 0.0 copy-done.1
  8.1 0.7 %shard_map.105 = (f32[16,3,16,128]{3,2,1,0:T(8,128)S(1)}, f32[3,16,256]{2,1,0:T(8,128)S(1)}, bf16[8,5,16,128]{3,2,1,0:T(8,128)(2,1)S(1)}, f32[8,16,128]{2,1,0:T(8,128)S(1)}, f32[8,16,128]{2,1,0:T(8,128)S(1)}) custom-call(s32[1,512]{1,0:T(1,128)S(1)} %get-tuple-element.34.refs_0_, f32[3,512]{1,0:T(4,128)S(1)} %bitcast.9, ...), custom_call_target="tpu_custom_call" | custom-call | flops 1000000000 | bytes 737280 | tf_op jit(solution)/shard_map/pallas_call | solution.py:118
  8.8 0.0 collective-permute-done.from_far
  8.9 1.9 %collective-permute-done.1.from_near = bf16[5,16,128]{2,1,0:T(8,128)(2,1)S(1)} collective-permute-done((bf16[5,16,128]{2,1,0:T(8,128)(2,1)S(1)}, bf16[5,16,128]{2,1,0:T(8,128)(2,1)S(1)}, u32[]{:S(2)}, u32[]{:S(2)}) %collective-permute-start.1) | collective-permute-done | bytes 20512 | tf_op jit(solution)/shard_map/ppermute | solution.py:519
  10.7 0.0 copy-start
  10.7 0.1 shard_map.106
  10.9 7.8 %collective-permute-start.2 = (bf16[26,16,128]{2,1,0:T(8,128)(2,1)S(1)}, bf16[26,16,128]{2,1,0:T(8,128)(2,1)S(1)}, u32[]{:S(2)}, u32[]{:S(2)}) collective-permute-start(bf16[26,16,128]{2,1,0:T(8,128)(2,1)S(1)} %get-tuple-element.51), channel_id=1, source_target_pairs={{1,2},{2,1},{3,4},{4,3},{5,6},{6,5},{7,8},{8,7},{9,10},{10,9},{11,... | collective-permute-start | bytes 319496 | tf_op jit(solution)/shard_map/ppermute | solution.py:519
  18.7 5.4 %collective-permute-start.3 = (bf16[26,16,128]{2,1,0:T(8,128)(2,1)S(1)}, bf16[26,16,128]{2,1,0:T(8,128)(2,1)S(1)}, u32[]{:S(2)}, u32[]{:S(2)}) collective-permute-start(bf16[26,16,128]{2,1,0:T(8,128)(2,1)S(1)} %get-tuple-element.52), channel_id=1, source_target_pairs={{0,1},{1,0},{2,3},{3,2},{4,5},{5,4},{6,7},{7,6},{8,9},{9,8},{10,11... | collective-permute-start | bytes 319496 | tf_op jit(solution)/shard_map/ppermute | solution.py:519
  24.1 0.0 copy-done
  24.1 0.0 copy-start.2
  24.1 0.0 copy-start.3
  24.2 0.0 copy-start.4
  24.2 1.0 %shard_map.107 = (f32[16,16,128]{2,1,0:T(8,128)S(1)}, f32[16,256]{1,0:T(8,128)S(1)}) custom-call(s32[1,4096]{1,0:T(1,128)S(1)} %bitcast.8), custom_call_target="tpu_custom_call" | custom-call | flops 1000000000 | bytes 147456 | tf_op jit(solution)/shard_map/pallas_call | solution.py:118
  25.2 0.0 collective-permute-done.2.refs_5_
  25.2 0.0 collective-permute-done.3.refs_6_
  25.2 0.0 copy-done.2
  25.2 0.0 copy-done.3
  25.2 0.0 copy-done.4
  25.2 3.4 %shard_map.108 = (bf16[384,128]{1,0:T(8,128)(2,1)}, f32[128,128]{1,0:T(8,128)}) custom-call(bf16[8,5,16,128]{3,2,1,0:T(8,128)(2,1)S(1)} %get-tuple-element.46.refs_0_, f32[8,16,128]{2,1,0:T(8,128)S(1)} %get-tuple-element.47.refs_1_, f32[8,16,128]{2,1,0:T(8,128)S(1)} %get-tuple-element.48.refs_2_, bf16[5,16,128]{2,1,0:T(8,128)(2,1)S(1)} %get-tuple-element.49.refs_3_, ...), custom_call_target="tpu_custom_call" | custom-call | flops 10000000000 | bytes 163840 | tf_op jit(solution)/shard_map/pallas_call | solution.py:118
Async XLA Ops:
  1.8 6.4 %copy-start.1 = (f32[512,3]{0,1:T(4,128)S(1)}, f32[512,3]{0,1:T(4,128)}, u32[]{:S(2)}) copy-start(f32[512,3]{0,1:T(4,128)} %param.14) | copy-start | bytes 18436
  1.8 7.1 %collective-permute-start = (bf16[5,16,128]{2,1,0:T(8,128)(2,1)S(1)}, bf16[5,16,128]{2,1,0:T(8,128)(2,1)S(1)}, u32[]{:S(2)}, u32[]{:S(2)}) collective-permute-start(bf16[5,16,128]{2,1,0:T(8,128)(2,1)S(1)} %get-tuple-element.32), channel_id=1, source_target_pairs={{32,64},{64,32},{96,128},{128,96},{160,192},{192,160},{224,256},{2... | collective-permute-start | bytes 61448 | tf_op jit(solution)/shard_map/ppermute | solution.py:519
  6.2 4.5 %collective-permute-start.1 = (bf16[5,16,128]{2,1,0:T(8,128)(2,1)S(1)}, bf16[5,16,128]{2,1,0:T(8,128)(2,1)S(1)}, u32[]{:S(2)}, u32[]{:S(2)}) collective-permute-start(bf16[5,16,128]{2,1,0:T(8,128)(2,1)S(1)} %get-tuple-element.33), channel_id=1, source_target_pairs={{0,32},{32,0},{64,96},{96,64},{128,160},{160,128},{192,224},{224,1... | collective-permute-start | bytes 61448 | tf_op jit(solution)/shard_map/ppermute | solution.py:519
  10.7 13.4 %copy-start = (s32[4096]{0:T(1024)S(1)}, s32[4096]{0:T(1024)}, u32[]{:S(2)}) copy-start(s32[4096]{0:T(1024)} %param.12) | copy-start | bytes 49156
  10.9 14.3 %collective-permute-start.2 = (bf16[26,16,128]{2,1,0:T(8,128)(2,1)S(1)}, bf16[26,16,128]{2,1,0:T(8,128)(2,1)S(1)}, u32[]{:S(2)}, u32[]{:S(2)}) collective-permute-start(bf16[26,16,128]{2,1,0:T(8,128)(2,1)S(1)} %get-tuple-element.51), channel_id=1, source_target_pairs={{1,2},{2,1},{3,4},{4,3},{5,6},{6,5},{7,8},{8,7},{9,10},{10,9},{11,... | collective-permute-start | bytes 319496 | tf_op jit(solution)/shard_map/ppermute | solution.py:519
  18.7 6.5 %collective-permute-start.3 = (bf16[26,16,128]{2,1,0:T(8,128)(2,1)S(1)}, bf16[26,16,128]{2,1,0:T(8,128)(2,1)S(1)}, u32[]{:S(2)}, u32[]{:S(2)}) collective-permute-start(bf16[26,16,128]{2,1,0:T(8,128)(2,1)S(1)} %get-tuple-element.52), channel_id=1, source_target_pairs={{0,1},{1,0},{2,3},{3,2},{4,5},{5,4},{6,7},{7,6},{8,9},{9,8},{10,11... | collective-permute-start | bytes 319496 | tf_op jit(solution)/shard_map/ppermute | solution.py:519
  24.1 1.1 %copy-start.2 = (bf16[1536,128]{1,0:T(8,128)(2,1)S(1)}, bf16[1536,128]{1,0:T(8,128)(2,1)}, u32[]{:S(2)}) copy-start(bf16[1536,128]{1,0:T(8,128)(2,1)} %constant.8.clone.refs_15_) | copy-start | bytes 1179652
  24.1 1.1 %copy-start.3 = (bf16[384,192]{1,0:T(8,128)(2,1)S(1)}, bf16[384,192]{1,0:T(8,128)(2,1)}, u32[]{:S(2)}) copy-start(bf16[384,192]{1,0:T(8,128)(2,1)} %constant.6.clone.refs_13_) | copy-start | bytes 442372
  24.2 1.1 %copy-start.4 = (bf16[96,48]{1,0:T(8,128)(2,1)S(1)}, bf16[96,48]{1,0:T(8,128)(2,1)}, u32[]{:S(2)}) copy-start(bf16[96,48]{1,0:T(8,128)(2,1)} %constant.7.clone.refs_14_) | copy-start | bytes 27652

commit v5 on v4

--- a/solution.py
+++ b/solution.py
@@ -21,7 +21,7 @@
 WIDE, SLOT, SEAM = 256, 117, 120
 OWN = COLS - SLOT
 PARTS = 2
-UNROLL = (8, 7, 6)
+LAG, AT, LAST = (8, 15), (3, 11, 18), 21
 KLASS = (0, 1, 2, 4, 5, 8)
 
 
@@ -256,13 +256,13 @@
     return (iota((rows, key.shape[1]), 0) == key).astype(F32).astype(BF16)
 
 
-def places(grid_y, grid_x, flat):
+def places(grid_y, grid_x, flat, slots):
     y0, x0 = starts()
     x = (flat & (grid_x - 1)) - x0
     y = ((flat // grid_x) & (grid_y - 1)) - y0 + LOW
     z = flat // (grid_x * grid_y)
     slot = jnp.where((x >= SLOT) & (x < SLOT + 16), x - SLOT, -1)
-    along = jnp.concatenate([one_hot(x + LOW, COLS), one_hot(slot, COLS)], axis=0)
+    along = jnp.concatenate([one_hot(x + LOW, COLS), one_hot(slot, slots)], axis=0)
     return along, y * DEPTH + z
 
 
@@ -288,7 +288,7 @@
         for p, plane in enumerate(planes):
             tiles[y, p] = plane.astype(BF16)
         st_own[y], co_own[y] = planes[3:]
-    at_x, ky = places(grid_y, grid_x, nodes[...])
+    at_x, ky = places(grid_y, grid_x, nodes[...], COLS)
     here = iota((256, ky.shape[1]), 0) == ky
     for c in range(3):
         force = forces[c : c + 1, :]
@@ -302,11 +302,11 @@
 
 def mask_body(grid_y, grid_x, fixed, free, free_b, spread):
     count = fixed.shape[1]
-    part = 512
+    part = 1024
     spread[...] = jnp.zeros_like(spread)
     for at in range(0, count, part):
-        kx, ky = places(grid_y, grid_x, fixed[:, at : at + part])
-        spread[...] += dots(one_hot(ky, 256), kx)
+        kx, ky = places(grid_y, grid_x, fixed[:, at : at + part], 16)
+        spread[:, : COLS + 16] += dots(one_hot(ky, 256), kx)
     free[...], free_b[...] = split(jnp.where(spread[...] > 0.0, 0.0, 1.0))
 
 
@@ -427,18 +427,6 @@
         return after, weight
 
     zero = jnp.zeros((2, 48, COLS), F32)
-    lax.fori_loop(
-        0,
-        8,
-        lambda i, c: first_pair(2 * i, c),
-        (zero, jnp.zeros((DEPTH, COLS), F32)),
-        unroll=UNROLL[0],
-    )
-    here_b = st_b + pltpu.roll(st_b, 1, 0)
-    inv_b = invert(here_b + pltpu.roll(here_b, 16, 1))
-    res_b = (loads_b[...] - forces_slots(ub[...]).reshape(3, DEPTH, WIDE)) * free_b[...][None]
-    put_slots(sb, step_of(res_b, inv_b), None)
-
     def second_pair(row, carry):
         applied, after = forces(ss, row, carry)
         for i in range(2):
@@ -447,9 +435,41 @@
             put(vv, row + i, new)
         return after
 
-    lax.fori_loop(0, 7, lambda i, c: second_pair(2 * i + 1, c), zero, unroll=UNROLL[1])
-    new_b = renew(ub[0:48, :], sb[0:48, :], res_b, forces_slots(sb[...]), free_b[...], inv_b)
-    put_slots(vb, new_b, None)
+    def energy(x):
+        f = jnp.dot(matrix[...], x, preferred_element_type=F32).reshape(2, 12, DEPTH, WIDE)
+        u = x.astype(F32).reshape(12, DEPTH, WIDE)
+        over = jnp.sum(f[1] * u, axis=0)
+        return jnp.sum(f[0] * u, axis=0) + pltpu.roll(over, DEPTH - 1, 0)
+
+    def energy_pair(row, carry):
+        value = energy(two(vv, row))
+        for i in range(2):
+            at = row + i - 2
+            ratio[at, :, 0:COLS] = value[:, i * COLS : (i + 1) * COLS] * co[at] * inverse[at]
+        return carry
+
+    carry, other_carry = (zero, jnp.zeros((DEPTH, COLS), F32)), zero
+    for turn in range(LAST):
+        if turn < 8:
+            carry = first_pair(2 * turn, carry)
+        if turn == AT[0]:
+            here_b = st_b + pltpu.roll(st_b, 1, 0)
+            inv_b = invert(here_b + pltpu.roll(here_b, 16, 1))
+            res_b = (loads_b[...] - forces_slots(ub[...]).reshape(3, DEPTH, WIDE)) * free_b[...][None]
+            put_slots(sb, step_of(res_b, inv_b), None)
+        if 0 <= turn - LAG[0] < 7:
+            other_carry = second_pair(2 * (turn - LAG[0]) + 1, other_carry)
+        if turn == AT[1]:
+            new_b = renew(ub[0:48, :], sb[0:48, :], res_b, forces_slots(sb[...]), free_b[...], inv_b)
+            put_slots(vb, new_b, None)
+        if 0 <= turn - LAG[1] < 6:
+            energy_pair(2 * (turn - LAG[1]) + 2, 0)
+        if turn == AT[2]:
+            ratio_b = energy(vb[...]) * co_b * inverse_b[...]
+    for at in range(12):
+        row = at + 2
+        part = ratio_b[:, (row // 8) * COLS : (row // 8 + 1) * COLS]
+        ratio[at, :, COLS:WIDE] = pltpu.roll(part, (COLS - 16 * (row % 8)) % COLS, 1)
 
     for y in range(ROWS):
         row, half = y + LOW, (y + LOW) // 8
@@ -460,26 +480,6 @@
         for c in range(3):
             out_f[pl.ds(c * 128 + y, DEPTH, stride=ROWS), :] = own[c * 16 : c * 16 + 16]
     smoothed[...] = out_f[...].astype(BF16)
-
-    def energy(x):
-        f = jnp.dot(matrix[...], x, preferred_element_type=F32).reshape(2, 12, DEPTH, WIDE)
-        u = x.astype(F32).reshape(12, DEPTH, WIDE)
-        over = jnp.sum(f[1] * u, axis=0)
-        return jnp.sum(f[0] * u, axis=0) + pltpu.roll(over, DEPTH - 1, 0)
-
-    def energy_pair(row, carry):
-        value = energy(two(vv, row))
-        for i in range(2):
-            at = row + i - 2
-            ratio[at, :, 0:COLS] = value[:, i * COLS : (i + 1) * COLS] * co[at] * inverse[at]
-        return carry
-
-    lax.fori_loop(0, 6, lambda i, c: energy_pair(2 * i + 2, c), 0, unroll=UNROLL[2])
-    ratio_b = energy(vb[...]) * co_b * inverse_b[...]
-    for at in range(12):
-        row = at + 2
-        part = ratio_b[:, (row // 8) * COLS : (row // 8 + 1) * COLS]
-        ratio[at, :, COLS:WIDE] = pltpu.roll(part, (COLS - 16 * (row % 8)) % COLS, 1)
 
     for y in range(ROWS):
         a = jnp.concatenate(

time: 28.9 us -> 28.6 us (0.990)
  Pallas kernels: 6.36 us -> 5.96 us
    pallas_call x5, Pallas kernels: 6.36 us -> 5.96 us  [call(): pl.pallas_call(body, out_shape=outs, in_specs=[pl.BlockSpec(memory_space=...]
where the time goes in v5:
time: 28.6 us; the launch traced here: 28.3 us
  starting transfers between devices  19.6 us (69%)
  Pallas kernels  5.96 us (21%)
  waiting for transfers between devices  1.88 us (7%)
  between operations  0.75 us (3%)
    ppermute x4, starting transfers between devices, swapped(): lax.ppermute(shard, axis, [(i, j) for i, j in enumerate(partner) if 0 <=...  19.6 us
    pallas_call x5, Pallas kernels, call(): pl.pallas_call(body, out_shape=outs, in_specs=[pl.BlockSpec(memory_space=...  5.96 us
    ppermute x4, waiting for transfers between devices, swapped(): lax.ppermute(shard, axis, [(i, j) for i, j in enumerate(partner) if 0 <=...  1.88 us
  transfers between devices with their start and end apart: 4, of which 1 were waited for; matrix products, arithmetic and copies ran while one was open for 0% of the time, Pallas kernels for 6%

profile of v5, /device:TPU:31, one launch (start us, length us, event | category | flops | bytes accessed | tf_op | source)
XLA Modules:
  0.0 28.3 jit_solution(131629532272586382)
XLA Ops:
  0.6 1.1 %shard_map.104 = (bf16[8,3,16,128]{3,2,1,0:T(8,128)(2,1)S(1)}, f32[8,16,128]{2,1,0:T(8,128)S(1)}, f32[8,16,128]{2,1,0:T(8,128)S(1)}, f32[8,16,128]{2,1,0:T(8,128...) custom-call(bf16[384,128]{1,0:T(8,128)(2,1)} %bitcast.10, ...), custom_call_target="tpu_custom_call" | custom-call | bytes 473088 | tf_op jit(solution)/shard_map/pallas_call | solution.py:118
  1.8 0.0 copy-start.1
  1.8 4.4 %collective-permute-start = (bf16[5,16,128]{2,1,0:T(8,128)(2,1)S(1)}, bf16[5,16,128]{2,1,0:T(8,128)(2,1)S(1)}, u32[]{:S(2)}, u32[]{:S(2)}) collective-permute-start(bf16[5,16,128]{2,1,0:T(8,128)(2,1)S(1)} %get-tuple-element.32), channel_id=1, source_target_pairs={{32,64},{64,32},{96,128},{128,96},{160,192},{192,160},{224,256},{2... | collective-permute-start | bytes 61448 | tf_op jit(solution)/shard_map/ppermute | solution.py:519
  6.2 1.9 %collective-permute-start.1 = (bf16[5,16,128]{2,1,0:T(8,128)(2,1)S(1)}, bf16[5,16,128]{2,1,0:T(8,128)(2,1)S(1)}, u32[]{:S(2)}, u32[]{:S(2)}) collective-permute-start(bf16[5,16,128]{2,1,0:T(8,128)(2,1)S(1)} %get-tuple-element.33), channel_id=1, source_target_pairs={{0,32},{32,0},{64,96},{96,64},{128,160},{160,128},{192,224},{224,1... | collective-permute-start | bytes 61448 | tf_op jit(solution)/shard_map/ppermute | solution.py:519
  8.1 0.0 copy-done.1
  8.1 0.7 %shard_map.105 = (f32[16,3,16,128]{3,2,1,0:T(8,128)S(1)}, f32[3,16,256]{2,1,0:T(8,128)S(1)}, bf16[8,5,16,128]{3,2,1,0:T(8,128)(2,1)S(1)}, f32[8,16,128]{2,1,0:T(8,128)S(1)}, f32[8,16,128]{2,1,0:T(8,128)S(1)}) custom-call(s32[1,512]{1,0:T(1,128)S(1)} %get-tuple-element.34.refs_0_, f32[3,512]{1,0:T(4,128)S(1)} %bitcast.9, ...), custom_call_target="tpu_custom_call" | custom-call | flops 1000000000 | bytes 737280 | tf_op jit(solution)/shard_map/pallas_call | solution.py:118
  8.8 0.0 collective-permute-done.from_far
  8.9 1.9 %collective-permute-done.1.from_near = bf16[5,16,128]{2,1,0:T(8,128)(2,1)S(1)} collective-permute-done((bf16[5,16,128]{2,1,0:T(8,128)(2,1)S(1)}, bf16[5,16,128]{2,1,0:T(8,128)(2,1)S(1)}, u32[]{:S(2)}, u32[]{:S(2)}) %collective-permute-start.1) | collective-permute-done | bytes 20512 | tf_op jit(solution)/shard_map/ppermute | solution.py:519
  10.7 0.0 copy-start
  10.7 0.1 shard_map.106
  10.9 7.8 %collective-permute-start.2 = (bf16[26,16,128]{2,1,0:T(8,128)(2,1)S(1)}, bf16[26,16,128]{2,1,0:T(8,128)(2,1)S(1)}, u32[]{:S(2)}, u32[]{:S(2)}) collective-permute-start(bf16[26,16,128]{2,1,0:T(8,128)(2,1)S(1)} %get-tuple-element.51), channel_id=1, source_target_pairs={{1,2},{2,1},{3,4},{4,3},{5,6},{6,5},{7,8},{8,7},{9,10},{10,9},{11,... | collective-permute-start | bytes 319496 | tf_op jit(solution)/shard_map/ppermute | solution.py:519
  18.7 5.4 %collective-permute-start.3 = (bf16[26,16,128]{2,1,0:T(8,128)(2,1)S(1)}, bf16[26,16,128]{2,1,0:T(8,128)(2,1)S(1)}, u32[]{:S(2)}, u32[]{:S(2)}) collective-permute-start(bf16[26,16,128]{2,1,0:T(8,128)(2,1)S(1)} %get-tuple-element.52), channel_id=1, source_target_pairs={{0,1},{1,0},{2,3},{3,2},{4,5},{5,4},{6,7},{7,6},{8,9},{9,8},{10,11... | collective-permute-start | bytes 319496 | tf_op jit(solution)/shard_map/ppermute | solution.py:519
  24.1 0.0 copy-done
  24.1 0.0 copy-start.2
  24.1 0.0 copy-start.3
  24.2 0.0 copy-start.4
  24.2 0.9 %shard_map.107 = (f32[16,16,128]{2,1,0:T(8,128)S(1)}, f32[16,256]{1,0:T(8,128)S(1)}) custom-call(s32[1,4096]{1,0:T(1,128)S(1)} %bitcast.8), custom_call_target="tpu_custom_call" | custom-call | flops 1000000000 | bytes 147456 | tf_op jit(solution)/shard_map/pallas_call | solution.py:118
  25.1 0.0 collective-permute-done.2.refs_5_
  25.1 0.0 collective-permute-done.3.refs_6_
  25.1 0.0 copy-done.2
  25.1 0.0 copy-done.3
  25.2 0.0 copy-done.4
  25.2 3.1 %shard_map.108 = (bf16[384,128]{1,0:T(8,128)(2,1)}, f32[128,128]{1,0:T(8,128)}) custom-call(bf16[8,5,16,128]{3,2,1,0:T(8,128)(2,1)S(1)} %get-tuple-element.46.refs_0_, f32[8,16,128]{2,1,0:T(8,128)S(1)} %get-tuple-element.47.refs_1_, f32[8,16,128]{2,1,0:T(8,128)S(1)} %get-tuple-element.48.refs_2_, bf16[5,16,128]{2,1,0:T(8,128)(2,1)S(1)} %get-tuple-element.49.refs_3_, ...), custom_call_target="tpu_custom_call" | custom-call | flops 10000000000 | bytes 163840 | tf_op jit(solution)/shard_map/pallas_call | solution.py:118
Async XLA Ops:
  1.8 6.4 %copy-start.1 = (f32[512,3]{0,1:T(4,128)S(1)}, f32[512,3]{0,1:T(4,128)}, u32[]{:S(2)}) copy-start(f32[512,3]{0,1:T(4,128)} %param.14) | copy-start | bytes 18436
  1.8 7.1 %collective-permute-start = (bf16[5,16,128]{2,1,0:T(8,128)(2,1)S(1)}, bf16[5,16,128]{2,1,0:T(8,128)(2,1)S(1)}, u32[]{:S(2)}, u32[]{:S(2)}) collective-permute-start(bf16[5,16,128]{2,1,0:T(8,128)(2,1)S(1)} %get-tuple-element.32), channel_id=1, source_target_pairs={{32,64},{64,32},{96,128},{128,96},{160,192},{192,160},{224,256},{2... | collective-permute-start | bytes 61448 | tf_op jit(solution)/shard_map/ppermute | solution.py:519
  6.2 4.5 %collective-permute-start.1 = (bf16[5,16,128]{2,1,0:T(8,128)(2,1)S(1)}, bf16[5,16,128]{2,1,0:T(8,128)(2,1)S(1)}, u32[]{:S(2)}, u32[]{:S(2)}) collective-permute-start(bf16[5,16,128]{2,1,0:T(8,128)(2,1)S(1)} %get-tuple-element.33), channel_id=1, source_target_pairs={{0,32},{32,0},{64,96},{96,64},{128,160},{160,128},{192,224},{224,1... | collective-permute-start | bytes 61448 | tf_op jit(solution)/shard_map/ppermute | solution.py:519
  10.7 13.4 %copy-start = (s32[4096]{0:T(1024)S(1)}, s32[4096]{0:T(1024)}, u32[]{:S(2)}) copy-start(s32[4096]{0:T(1024)} %param.12) | copy-start | bytes 49156
  10.9 14.2 %collective-permute-start.2 = (bf16[26,16,128]{2,1,0:T(8,128)(2,1)S(1)}, bf16[26,16,128]{2,1,0:T(8,128)(2,1)S(1)}, u32[]{:S(2)}, u32[]{:S(2)}) collective-permute-start(bf16[26,16,128]{2,1,0:T(8,128)(2,1)S(1)} %get-tuple-element.51), channel_id=1, source_target_pairs={{1,2},{2,1},{3,4},{4,3},{5,6},{6,5},{7,8},{8,7},{9,10},{10,9},{11,... | collective-permute-start | bytes 319496 | tf_op jit(solution)/shard_map/ppermute | solution.py:519
  18.7 6.4 %collective-permute-start.3 = (bf16[26,16,128]{2,1,0:T(8,128)(2,1)S(1)}, bf16[26,16,128]{2,1,0:T(8,128)(2,1)S(1)}, u32[]{:S(2)}, u32[]{:S(2)}) collective-permute-start(bf16[26,16,128]{2,1,0:T(8,128)(2,1)S(1)} %get-tuple-element.52), channel_id=1, source_target_pairs={{0,1},{1,0},{2,3},{3,2},{4,5},{5,4},{6,7},{7,6},{8,9},{9,8},{10,11... | collective-permute-start | bytes 319496 | tf_op jit(solution)/shard_map/ppermute | solution.py:519
  24.1 1.0 %copy-start.2 = (bf16[1536,128]{1,0:T(8,128)(2,1)S(1)}, bf16[1536,128]{1,0:T(8,128)(2,1)}, u32[]{:S(2)}) copy-start(bf16[1536,128]{1,0:T(8,128)(2,1)} %constant.8.clone.refs_15_) | copy-start | bytes 1179652
  24.1 1.0 %copy-start.3 = (bf16[384,192]{1,0:T(8,128)(2,1)S(1)}, bf16[384,192]{1,0:T(8,128)(2,1)}, u32[]{:S(2)}) copy-start(bf16[384,192]{1,0:T(8,128)(2,1)} %constant.6.clone.refs_13_) | copy-start | bytes 442372
  24.2 1.0 %copy-start.4 = (bf16[96,48]{1,0:T(8,128)(2,1)S(1)}, bf16[96,48]{1,0:T(8,128)(2,1)}, u32[]{:S(2)}) copy-start(bf16[96,48]{1,0:T(8,128)(2,1)} %constant.7.clone.refs_14_) | copy-start | bytes 27652

commit v6 on v5

--- a/solution.py
+++ b/solution.py
@@ -302,7 +302,7 @@
 
 def mask_body(grid_y, grid_x, fixed, free, free_b, spread):
     count = fixed.shape[1]
-    part = 1024
+    part = 2048
     spread[...] = jnp.zeros_like(spread)
     for at in range(0, count, part):
         kx, ky = places(grid_y, grid_x, fixed[:, at : at + part], 16)

time: 28.6 us -> 28.6 us (level)
  no operation moved by 1% of the time
where the time goes in v6:
time: 28.6 us; the launch traced here: 28.3 us
  starting transfers between devices  19.6 us (69%)
  Pallas kernels  5.92 us (21%)
  waiting for transfers between devices  1.89 us (7%)
  between operations  0.75 us (3%)
    ppermute x4, starting transfers between devices, swapped(): lax.ppermute(shard, axis, [(i, j) for i, j in enumerate(partner) if 0 <=...  19.6 us
    pallas_call x5, Pallas kernels, call(): pl.pallas_call(body, out_shape=outs, in_specs=[pl.BlockSpec(memory_space=...  5.92 us
    ppermute x4, waiting for transfers between devices, swapped(): lax.ppermute(shard, axis, [(i, j) for i, j in enumerate(partner) if 0 <=...  1.89 us
  transfers between devices with their start and end apart: 4, of which 1 were waited for; matrix products, arithmetic and copies ran while one was open for 0% of the time, Pallas kernels for 6%

profile of v6, /device:TPU:31, one launch (start us, length us, event | category | flops | bytes accessed | tf_op | source)
XLA Modules:
  0.0 28.3 jit_solution(12575587286933767400)
XLA Ops:
  0.6 1.1 %shard_map.104 = (bf16[8,3,16,128]{3,2,1,0:T(8,128)(2,1)S(1)}, f32[8,16,128]{2,1,0:T(8,128)S(1)}, f32[8,16,128]{2,1,0:T(8,128)S(1)}, f32[8,16,128]{2,1,0:T(8,128...) custom-call(bf16[384,128]{1,0:T(8,128)(2,1)} %bitcast.10, ...), custom_call_target="tpu_custom_call" | custom-call | bytes 473088 | tf_op jit(solution)/shard_map/pallas_call | solution.py:118
  1.8 0.0 copy-start.1
  1.8 4.4 %collective-permute-start = (bf16[5,16,128]{2,1,0:T(8,128)(2,1)S(1)}, bf16[5,16,128]{2,1,0:T(8,128)(2,1)S(1)}, u32[]{:S(2)}, u32[]{:S(2)}) collective-permute-start(bf16[5,16,128]{2,1,0:T(8,128)(2,1)S(1)} %get-tuple-element.32), channel_id=1, source_target_pairs={{32,64},{64,32},{96,128},{128,96},{160,192},{192,160},{224,256},{2... | collective-permute-start | bytes 61448 | tf_op jit(solution)/shard_map/ppermute | solution.py:519
  6.2 1.9 %collective-permute-start.1 = (bf16[5,16,128]{2,1,0:T(8,128)(2,1)S(1)}, bf16[5,16,128]{2,1,0:T(8,128)(2,1)S(1)}, u32[]{:S(2)}, u32[]{:S(2)}) collective-permute-start(bf16[5,16,128]{2,1,0:T(8,128)(2,1)S(1)} %get-tuple-element.33), channel_id=1, source_target_pairs={{0,32},{32,0},{64,96},{96,64},{128,160},{160,128},{192,224},{224,1... | collective-permute-start | bytes 61448 | tf_op jit(solution)/shard_map/ppermute | solution.py:519
  8.1 0.0 copy-done.1
  8.1 0.7 %shard_map.105 = (f32[16,3,16,128]{3,2,1,0:T(8,128)S(1)}, f32[3,16,256]{2,1,0:T(8,128)S(1)}, bf16[8,5,16,128]{3,2,1,0:T(8,128)(2,1)S(1)}, f32[8,16,128]{2,1,0:T(8,128)S(1)}, f32[8,16,128]{2,1,0:T(8,128)S(1)}) custom-call(s32[1,512]{1,0:T(1,128)S(1)} %get-tuple-element.34.refs_0_, f32[3,512]{1,0:T(4,128)S(1)} %bitcast.9, ...), custom_call_target="tpu_custom_call" | custom-call | flops 1000000000 | bytes 737280 | tf_op jit(solution)/shard_map/pallas_call | solution.py:118
  8.8 0.0 collective-permute-done.from_far
  8.9 1.9 %collective-permute-done.1.from_near = bf16[5,16,128]{2,1,0:T(8,128)(2,1)S(1)} collective-permute-done((bf16[5,16,128]{2,1,0:T(8,128)(2,1)S(1)}, bf16[5,16,128]{2,1,0:T(8,128)(2,1)S(1)}, u32[]{:S(2)}, u32[]{:S(2)}) %collective-permute-start.1) | collective-permute-done | bytes 20512 | tf_op jit(solution)/shard_map/ppermute | solution.py:519
  10.7 0.0 copy-start
  10.7 0.1 shard_map.106
  10.9 7.8 %collective-permute-start.2 = (bf16[26,16,128]{2,1,0:T(8,128)(2,1)S(1)}, bf16[26,16,128]{2,1,0:T(8,128)(2,1)S(1)}, u32[]{:S(2)}, u32[]{:S(2)}) collective-permute-start(bf16[26,16,128]{2,1,0:T(8,128)(2,1)S(1)} %get-tuple-element.51), channel_id=1, source_target_pairs={{1,2},{2,1},{3,4},{4,3},{5,6},{6,5},{7,8},{8,7},{9,10},{10,9},{11,... | collective-permute-start | bytes 319496 | tf_op jit(solution)/shard_map/ppermute | solution.py:519
  18.7 5.4 %collective-permute-start.3 = (bf16[26,16,128]{2,1,0:T(8,128)(2,1)S(1)}, bf16[26,16,128]{2,1,0:T(8,128)(2,1)S(1)}, u32[]{:S(2)}, u32[]{:S(2)}) collective-permute-start(bf16[26,16,128]{2,1,0:T(8,128)(2,1)S(1)} %get-tuple-element.52), channel_id=1, source_target_pairs={{0,1},{1,0},{2,3},{3,2},{4,5},{5,4},{6,7},{7,6},{8,9},{9,8},{10,11... | collective-permute-start | bytes 319496 | tf_op jit(solution)/shard_map/ppermute | solution.py:519
  24.1 0.0 copy-done
  24.1 0.0 copy-start.2
  24.1 0.0 copy-start.3
  24.2 0.0 copy-start.4
  24.2 0.9 %shard_map.107 = (f32[16,16,128]{2,1,0:T(8,128)S(1)}, f32[16,256]{1,0:T(8,128)S(1)}) custom-call(s32[1,4096]{1,0:T(1,128)S(1)} %bitcast.8), custom_call_target="tpu_custom_call" | custom-call | flops 1000000000 | bytes 147456 | tf_op jit(solution)/shard_map/pallas_call | solution.py:118
  25.0 0.0 collective-permute-done.2.refs_5_
  25.0 0.0 collective-permute-done.3.refs_6_
  25.1 0.1 copy-done.2
  25.1 0.0 copy-done.3
  25.2 0.0 copy-done.4
  25.2 3.1 %shard_map.108 = (bf16[384,128]{1,0:T(8,128)(2,1)}, f32[128,128]{1,0:T(8,128)}) custom-call(bf16[8,5,16,128]{3,2,1,0:T(8,128)(2,1)S(1)} %get-tuple-element.46.refs_0_, f32[8,16,128]{2,1,0:T(8,128)S(1)} %get-tuple-element.47.refs_1_, f32[8,16,128]{2,1,0:T(8,128)S(1)} %get-tuple-element.48.refs_2_, bf16[5,16,128]{2,1,0:T(8,128)(2,1)S(1)} %get-tuple-element.49.refs_3_, ...), custom_call_target="tpu_custom_call" | custom-call | flops 10000000000 | bytes 163840 | tf_op jit(solution)/shard_map/pallas_call | solution.py:118
Async XLA Ops:
  1.8 6.4 %copy-start.1 = (f32[512,3]{0,1:T(4,128)S(1)}, f32[512,3]{0,1:T(4,128)}, u32[]{:S(2)}) copy-start(f32[512,3]{0,1:T(4,128)} %param.14) | copy-start | bytes 18436
  1.8 7.1 %collective-permute-start = (bf16[5,16,128]{2,1,0:T(8,128)(2,1)S(1)}, bf16[5,16,128]{2,1,0:T(8,128)(2,1)S(1)}, u32[]{:S(2)}, u32[]{:S(2)}) collective-permute-start(bf16[5,16,128]{2,1,0:T(8,128)(2,1)S(1)} %get-tuple-element.32), channel_id=1, source_target_pairs={{32,64},{64,32},{96,128},{128,96},{160,192},{192,160},{224,256},{2... | collective-permute-start | bytes 61448 | tf_op jit(solution)/shard_map/ppermute | solution.py:519
  6.2 4.5 %collective-permute-start.1 = (bf16[5,16,128]{2,1,0:T(8,128)(2,1)S(1)}, bf16[5,16,128]{2,1,0:T(8,128)(2,1)S(1)}, u32[]{:S(2)}, u32[]{:S(2)}) collective-permute-start(bf16[5,16,128]{2,1,0:T(8,128)(2,1)S(1)} %get-tuple-element.33), channel_id=1, source_target_pairs={{0,32},{32,0},{64,96},{96,64},{128,160},{160,128},{192,224},{224,1... | collective-permute-start | bytes 61448 | tf_op jit(solution)/shard_map/ppermute | solution.py:519
  10.7 13.4 %copy-start = (s32[4096]{0:T(1024)S(1)}, s32[4096]{0:T(1024)}, u32[]{:S(2)}) copy-start(s32[4096]{0:T(1024)} %param.12) | copy-start | bytes 49156
  10.9 14.2 %collective-permute-start.2 = (bf16[26,16,128]{2,1,0:T(8,128)(2,1)S(1)}, bf16[26,16,128]{2,1,0:T(8,128)(2,1)S(1)}, u32[]{:S(2)}, u32[]{:S(2)}) collective-permute-start(bf16[26,16,128]{2,1,0:T(8,128)(2,1)S(1)} %get-tuple-element.51), channel_id=1, source_target_pairs={{1,2},{2,1},{3,4},{4,3},{5,6},{6,5},{7,8},{8,7},{9,10},{10,9},{11,... | collective-permute-start | bytes 319496 | tf_op jit(solution)/shard_map/ppermute | solution.py:519
  18.7 6.4 %collective-permute-start.3 = (bf16[26,16,128]{2,1,0:T(8,128)(2,1)S(1)}, bf16[26,16,128]{2,1,0:T(8,128)(2,1)S(1)}, u32[]{:S(2)}, u32[]{:S(2)}) collective-permute-start(bf16[26,16,128]{2,1,0:T(8,128)(2,1)S(1)} %get-tuple-element.52), channel_id=1, source_target_pairs={{0,1},{1,0},{2,3},{3,2},{4,5},{5,4},{6,7},{7,6},{8,9},{9,8},{10,11... | collective-permute-start | bytes 319496 | tf_op jit(solution)/shard_map/ppermute | solution.py:519
  24.1 1.0 %copy-start.2 = (bf16[1536,128]{1,0:T(8,128)(2,1)S(1)}, bf16[1536,128]{1,0:T(8,128)(2,1)}, u32[]{:S(2)}) copy-start(bf16[1536,128]{1,0:T(8,128)(2,1)} %constant.8.clone.refs_15_) | copy-start | bytes 1179652
  24.1 1.0 %copy-start.3 = (bf16[384,192]{1,0:T(8,128)(2,1)S(1)}, bf16[384,192]{1,0:T(8,128)(2,1)}, u32[]{:S(2)}) copy-start(bf16[384,192]{1,0:T(8,128)(2,1)} %constant.6.clone.refs_13_) | copy-start | bytes 442372
  24.2 1.0 %copy-start.4 = (bf16[96,48]{1,0:T(8,128)(2,1)S(1)}, bf16[96,48]{1,0:T(8,128)(2,1)}, u32[]{:S(2)}) copy-start(bf16[96,48]{1,0:T(8,128)(2,1)} %constant.7.clone.refs_14_) | copy-start | bytes 27652
